TPU v7x, 128 devices: a whole 4x4x4 slice. The times are simulated.
128 devices in a mesh: clip: 32 (over y, x, core), seq: 4 (over z).
Axes of the slice: x: 4, y: 4, z: 4, core: 2. Of those that a mesh axis runs over, the one named last changes fastest.
Arguments:
- vae_in: bfloat16 [512, 8, 32, 512], P('clip', 'seq'), may hold values from -6 to 6
- vae_gain: float32 [512], replicated, may hold values from 0.25 to 1.75
- w_conv: bfloat16 [3, 512, 512], replicated, may hold values from -0.15625 to 0.15625
- b_conv: float32 [512], replicated, may hold values from -3 to 3
- w_lat: bfloat16 [512, 16], replicated, may hold values from -0.25 to 0.25
- b_lat: float32 [16], replicated, may hold values from -3 to 3
- w_emb: bfloat16 [64, 3072], replicated, may hold values from -0.75 to 0.75
- b_emb: float32 [3072], replicated, may hold values from -3 to 3
- clip_lengths: int32 [64], replicated, may hold values from 6 to 8, as said below
- clip_owner: int32 [64], replicated, may hold values from 0 to 31
- clip_mod: float32 [64, 3, 3072], replicated, may hold values from -6 to 6
- w_qkv: bfloat16 [3072, 3, 3072], P(None, None, 'seq'), may hold values from -1 to 1
- w_out: bfloat16 [3072, 3072], P('seq'), may hold values from -0.109375 to 0.109375
Outputs:
- block_out: bfloat16 [512, 4, 16, 3072], P('clip', 'seq')
Inputs may be any that keep to these rules, and one draw needn't show every extreme that they name: `clip_lengths`: clips lie end to end from frame 0 in index order; frames after the last clip belong to no clip. Clip r * 32 + p is owned by a group that depends on p alone, so every group owns 2 clips; the clips of the group at p = 0 have 8 frames each, so that group owns 16 frames. Among the 16 frames of one index of clip, at most 8 belong to one group, and on index 0 that many do.
All inputs are finite; a program needn't handle non-finite values.
Results may differ from a plain program's by a relative error of at most 0.015.
Values may be sent and summed in bfloat16 or wider, within the bound.
A program may use at most 192 MiB of HBM per device.

v0:
```python
import math

import jax
import jax.numpy as jnp
from jax import lax
from jax.sharding import PartitionSpec as P

HD = 128
LEN_HI = 8


NEG = -1e30


def extended(array, sides, width):
    for axis, dim in sides:
        size, length = (lax.axis_size(axis), array.shape[dim])
        up = [(i, (i + 1) % size) for i in range(size - 1)]
        down = [(j, i) for i, j in up]
        last = lax.slice_in_dim(array, length - width, length, axis=dim)
        initial = lax.slice_in_dim(array, 0, width, axis=dim)
        before = lax.ppermute(last, axis, up)
        after = lax.ppermute(initial, axis, down)
        array = jnp.concatenate([before, array, after], axis=dim)
    return array


def frame_tables(clip_lengths, clip_owner, frames):
    count = clip_lengths.shape[0]
    ends = jnp.cumsum(clip_lengths)
    starts = ends - clip_lengths
    frame_ids = jnp.arange(frames, dtype=jnp.int32)
    inside = (frame_ids[:, None] >= starts[None, :]) & (frame_ids[:, None] < ends[None, :])
    inside_int = inside.astype(jnp.int32)
    live = jnp.sum(inside_int, axis=1) > 0
    clip_ids = jnp.arange(count, dtype=jnp.int32)
    same_owner = clip_owner[:, None] == clip_owner[None, :]
    earlier = clip_ids[:, None] > clip_ids[None, :]
    offset = jnp.sum(jnp.where(same_owner & earlier, clip_lengths[None, :], 0), axis=1)
    frame_clip = jnp.where(live, jnp.sum(inside_int * clip_ids[None, :], axis=1), -1)
    frame_owner = jnp.where(live, jnp.sum(inside_int * clip_owner[None, :], axis=1), -1)
    shifted = offset - starts
    frame_slot = jnp.where(live, jnp.sum(inside_int * shifted[None, :], axis=1) + frame_ids, -1)
    return (frame_clip, frame_owner, frame_slot)


def embed_rows(patches, w_emb, b_emb):
    return (jnp.dot(patches, w_emb, preferred_element_type=jnp.float32) + b_emb).astype(
        jnp.bfloat16
    )


def shards(
    vae_in,
    vae_gain,
    w_conv,
    b_conv,
    w_lat,
    b_lat,
    w_emb,
    b_emb,
    clip_lengths,
    clip_owner,
    clip_mod,
    w_qkv,
    w_out,
):
    groups = lax.axis_size("clip")
    regions = lax.axis_size("seq")
    slab = lax.axis_index("clip")
    region = lax.axis_index("seq")
    fr_slab, rows_dev, cols, channels = vae_in.shape
    frames = fr_slab * groups
    capacity = LEN_HI
    frame_clip, frame_owner, frame_slot = frame_tables(clip_lengths, clip_owner, frames)
    first = slab * fr_slab
    own_clip = lax.dynamic_slice_in_dim(frame_clip, first, fr_slab)
    own_group = lax.dynamic_slice_in_dim(frame_owner, first, fr_slab)
    own_slot = lax.dynamic_slice_in_dim(frame_slot, first, fr_slab)
    values = vae_in.astype(jnp.float32)
    power = jnp.mean(values * values, axis=-1, keepdims=True)
    act = jax.nn.silu(values * lax.rsqrt(power + 1e-06) * vae_gain).astype(jnp.bfloat16)
    padded = extended(act, (("clip", 0),), 1)
    border = jnp.full((1,), -2, jnp.int32)
    clip_pad = jnp.concatenate([border, frame_clip, border])
    conv = jnp.zeros(values.shape, jnp.float32) + b_conv
    for tap in range(3):
        near_clip = lax.dynamic_slice_in_dim(clip_pad, first + tap, fr_slab)
        keep = (near_clip == own_clip)[:, None, None, None]
        term = jnp.dot(padded[tap : tap + fr_slab], w_conv[tap], preferred_element_type=jnp.float32)
        conv = conv + jnp.where(keep, term, 0.0)
    resid = (values + conv).astype(jnp.bfloat16)
    latent = jnp.dot(resid, w_lat, preferred_element_type=jnp.float32) + b_lat
    latent = latent.reshape(fr_slab, rows_dev // 2, 2, cols // 2, 2, latent.shape[3])
    patches = (
        latent.transpose(0, 1, 3, 2, 4, 5)
        .reshape(fr_slab, rows_dev // 2 * (cols // 2), -1)
        .astype(jnp.bfloat16)
    )
    tok_frame = patches.shape[1]
    patch_width = patches.shape[2]
    rows = patches.reshape(fr_slab, -1)
    width = rows.shape[1]
    zero = jnp.zeros((), rows.dtype)
    group_ids = jnp.arange(groups, dtype=jnp.int32)
    onehot = (
        (frame_owner[:, None] == group_ids[None, :])
        .astype(jnp.int32)
        .reshape(groups, fr_slab, groups)
    )
    counts = jnp.sum(onehot, axis=1)
    before = jnp.cumsum(counts, axis=0) - counts
    mine_before = lax.dynamic_index_in_dim(before, slab, axis=0, keepdims=False)
    rank = own_slot[None, :] - mine_before[:, None]
    places = jnp.arange(capacity, dtype=jnp.int32)
    pick = (own_group[None, None, :] == group_ids[:, None, None]) & (
        rank[:, None, :] == places[None, :, None]
    )
    pick_int = pick.astype(jnp.int32)
    local_ids = jnp.arange(fr_slab, dtype=jnp.int32)
    source = jnp.sum(pick_int * local_ids, axis=-1)
    sent = jnp.sum(pick_int, axis=-1) > 0
    outgoing = jnp.take(rows, source.reshape(-1), axis=0).reshape(groups, capacity, width)
    outgoing = jnp.where(sent[:, :, None], outgoing, zero)
    slot_ids = jnp.arange(fr_slab, dtype=jnp.int32)
    frame_ids = jnp.arange(frames, dtype=jnp.int32)
    take_int = ((frame_owner[None, :] == slab) & (frame_slot[None, :] == slot_ids[:, None])).astype(
        jnp.int32
    )
    frame_of = jnp.sum(take_int * frame_ids, axis=-1)
    valid = jnp.sum(take_int, axis=-1) > 0
    slot_clip = jnp.where(valid, jnp.sum(take_int * frame_clip, axis=-1), -1)
    from_slab = frame_of // fr_slab
    column = lax.dynamic_index_in_dim(before, slab, axis=1, keepdims=False)
    offset = jnp.sum(
        jnp.where(from_slab[:, None] == group_ids[None, :], column[None, :], 0), axis=1
    )
    place = slot_ids - offset
    wide = jnp.broadcast_to(outgoing[:, None], (groups, regions, capacity, width)).reshape(
        groups * regions * capacity, width
    )
    arrived = lax.all_to_all(wide, ("clip", "seq"), split_axis=0, concat_axis=0, tiled=True)
    region_ids = jnp.arange(regions, dtype=jnp.int32)
    index = (from_slab[:, None] * regions + region_ids[None, :]) * capacity + place[:, None]
    index = jnp.where(valid[:, None], index, 0)
    every = jnp.take(arrived, index.reshape(-1), axis=0).reshape(fr_slab, regions, width)
    empty_tok = jnp.zeros((), jnp.bfloat16)
    tokens = embed_rows(every.reshape(fr_slab, regions * tok_frame, patch_width), w_emb, b_emb)
    tokens = jnp.where(valid[:, None, None], tokens, empty_tok)
    model = tokens.shape[2]
    tokg = fr_slab * regions * tok_frame
    mods = jnp.take(clip_mod, jnp.maximum(slot_clip, 0), axis=0)
    token_values = tokens.astype(jnp.float32)
    mean = jnp.mean(token_values, axis=-1, keepdims=True)
    centred = token_values - mean
    spread = jnp.mean(centred * centred, axis=-1, keepdims=True)
    normed = centred * lax.rsqrt(spread + 1e-06)
    hidden = normed * (1.0 + mods[:, None, 1, :]) + mods[:, None, 0, :]
    hidden = hidden.astype(jnp.bfloat16).reshape(tokg, model)
    head_width = w_qkv.shape[2]
    heads_dev = head_width // HD
    qkv = jnp.dot(
        hidden, w_qkv.reshape(model, 3 * head_width), preferred_element_type=jnp.float32
    ).astype(jnp.bfloat16)
    qkv = qkv.reshape(tokg, 3, heads_dev, HD)
    queries = qkv[:, 0]
    keys = qkv[:, 1]
    vals = qkv[:, 2]
    token_clip = jnp.repeat(slot_clip, regions * tok_frame, total_repeat_length=tokg)
    block = math.gcd(512, tokg)

    def one_block(start):
        query = lax.dynamic_slice_in_dim(queries, start, block, 0)
        query_clip = lax.dynamic_slice_in_dim(token_clip, start, block, 0)
        scores = jnp.einsum(
            "qhd,khd->hqk", query, keys, preferred_element_type=jnp.float32
        ) * HD ** (-0.5)
        same = (query_clip[:, None] == token_clip[None, :])[None]
        masked = jnp.where(same, scores, NEG)
        top = jnp.max(masked, axis=-1, keepdims=True)
        weights = jnp.exp(masked - top)
        probs = (weights / jnp.sum(weights, axis=-1, keepdims=True)).astype(jnp.bfloat16)
        return jnp.einsum("hqk,khd->qhd", probs, vals, preferred_element_type=jnp.float32).astype(
            jnp.bfloat16
        )

    block_starts = jnp.arange(tokg // block, dtype=jnp.int32) * block
    attended = lax.map(one_block, block_starts)
    attended = attended.reshape(fr_slab, regions, tok_frame, head_width)
    ordered = attended.transpose(1, 0, 2, 3).reshape(tokg, head_width)

    def term(start, count):
        piece = lax.dynamic_slice_in_dim(ordered, start, count, 0)
        return jnp.dot(piece, w_out, preferred_element_type=jnp.float32)

    proj = lax.psum_scatter(
        term(jnp.int32(0), lax.axis_size("seq") * (fr_slab * tok_frame)).astype(jnp.bfloat16),
        "seq",
        scatter_dimension=0,
        tiled=True,
    ).astype(jnp.float32)
    own = lax.dynamic_index_in_dim(
        token_values.reshape(fr_slab, regions, tok_frame, model), region, axis=1, keepdims=False
    )
    gate = mods[:, 2, :]
    out = own + gate[:, None, :] * proj.reshape(fr_slab, tok_frame, model)
    out = jnp.where(valid[:, None, None], out, 0.0).astype(jnp.bfloat16)
    return out.reshape(fr_slab, rows_dev // 2, cols // 2, model)


def solution(mesh):
    in_specs = (
        P("clip", "seq", None, None),
        P(),
        P(),
        P(),
        P(),
        P(),
        P(),
        P(),
        P(),
        P(),
        P(),
        P(None, None, "seq"),
        P("seq", None),
    )
    out_specs = P("clip", "seq", None, None)
    return jax.shard_map(shards, mesh=mesh, in_specs=in_specs, out_specs=out_specs, check_vma=False)
```

profile of v0, /device:TPU:1, one launch (start us, length us, event | category | flops | bytes accessed | tf_op | source)
XLA Modules:
  0.0 295.6 jit_solution(2124766956810769645)
XLA Ops:
  6.5 1.6 fusion.17
  8.2 1.9 fusion.24
  10.1 0.6 fusion.73
  10.8 4.5 %collective-permute-start = (bf16[1,2,32,512]{3,2,1,0:T(8,128)(2,1)}, bf16[1,2,32,512]{3,2,1,0:T(8,128)(2,1)}, u32[]{:S(2)}, u32[]{:S(2)}) collective-permute-start(bf16[1,2,32,512]{3,2,1,0:T(8,128)(2,1)} %get-tuple-element.119), channel_id=1, source_target_pairs={{0,4},{4,8},{8,12},{12,16},{16,20},{20,24},{24,28},{28,32},{32,36}... | collective-permute-start | bytes 196616 | tf_op jit(solution)/shard_map/ppermute | solution.py:22
  15.3 1.9 collective-permute-start.1
  17.5 0.2 select_reduce_fusion.6
  17.7 0.1 select_reduce_fusion.2
  18.0 0.2 convert_reduce_fusion.1
  18.2 0.2 dynamic-slice_reduce_fusion
  18.6 0.2 select_reduce_fusion.5
  18.7 0.5 broadcast_compare_fusion.4
  19.3 0.2 select_reduce_fusion.7
  19.6 0.6 compare_and_fusion
  20.3 3.1 %fusion.46 = f32[16,2,32,512]{3,2,1,0:T(8,128)} fusion(bf16[16,2,32,512]{3,2,1,0:T(8,128)(2,1)S(1)} %fusion.24, bf16[3,512,512]{2,1,0:T(8,128)(2,1)} %param.19), kind=kOutput, calls=%fused_computation.63 | convolution fusion | flops 536870912 | bytes 3670016 | tf_op jit(solution)/shard_map/dot_general | solution.py:90
  23.7 0.6 pad_clamp_fusion.2
  24.6 0.6 pad_clamp_fusion.1
  25.2 0.6 pad_clamp_fusion
  25.8 0.7 add_add_fusion.1
  26.5 0.7 dynamic-slice_compare_fusion.2
  27.1 3.1 %fusion.29 = f32[16,2,32,512]{3,2,1,0:T(8,128)} fusion(bf16[16,2,32,512]{3,2,1,0:T(8,128)(2,1)S(1)} %fusion.24, bf16[1,2,32,512]{3,2,1,0:T(8,128)(2,1)} %collective-permute-done, bf16[3,512,512]{2,1,0:T(8,128)(2,1)} %param.19), kind=kOutput, calls=%fused_computation.50 | convolution fusion | flops 539099136 | bytes 3735552 | tf_op jit(solution)/shard_map/dot_general | solution.py:90
  30.2 4.3 %fusion.28 = bf16[16,2,32,16]{2,3,1,0:T(8,128)(2,1)S(1)} fusion(bf16[16,2,32,512]{3,2,1,0:T(8,128)(2,1)} %param.17, f32[16,2,32,512]{3,2,1,0:T(8,128)} %fusion.46, f32[16,2,32,512]{3,2,1,0:T(8,128)} %fusion.29, bf16[1,2,32,512]{3,2,1,0:T(8,128)(2,1)} %collective-permute-done.1, bf16[16,2,32,512]{3,2,1,0:T(8,128)(2,1)S(1)} %fusion.24, f32[512]{0:T(512)} %param.20, ...), kind=kOutput, calls=%fused_computation.49 | convolution fusion | flops 560627712 | bytes 6934528 | tf_op jit(solution)/shard_map/dot_general | solution.py:93
  34.5 0.3 copy.34
  34.8 0.2 copy.35
  35.1 0.3 convert_element_type.74
  35.4 1.3 gather_fusion
  36.7 0.1 fusion.49
  36.8 1.6 broadcast_in_dim.251
  38.4 11.1 %all-to-all-start = ((bf16[128,8,1024]{2,1,0:T(8,128)(2,1)}), bf16[128,8,1024]{2,1,0:T(8,128)(2,1)}, u32[]{:S(2)}, u32[]{:S(2)}) async-start(bf16[128,8,1024]{2,1,0:T(8,128)(2,1)} %bitcast.125), calls=%async_computation | async-start | bytes 4194304 | tf_op jit(solution)/shard_map/all_to_all | solution.py:142
  49.5 0.2 reduce-scatter.2.cloned.1.call-start
  50.0 18.6 %copy.37 = bf16[3072,3,768]{0,2,1:T(8,128)(2,1)} copy(bf16[3072,3,768]{2,0,1:T(8,128)(2,1)} %param.28) | data formatting | bytes 28311552 | tf_op args[11]
  68.6 1.5 gather_fusion.2
  70.2 0.7 fusion.74
  70.9 4.5 %compare_select_fusion.2 = (s32[1024,1]{0,1:T(1,128)S(1)}, s32[1024,1]{0,1:T(1,128)S(1)}) fusion(s32[]{:T(128)} %bitcast.39, s32[]{:T(128)} %bitcast.40, s32[]{:T(128)} %bitcast.41, s32[]{:T(128)} %bitcast.42, s32[]{:T(128)} %bitcast.43, s32[]{:T(128)} %bitcast.45, s32[]{:T(128)} %bitcast.44, s32[1024,1]{0,1:T(1,128)S(1)} %bitcast.132, ...), kind=kLoop, calls=%fused_computation.115 | loop fusion | flops 14336 | bytes 16412 | tf_op jit(solution)/shard_map/jit(_take)/gather | solution.py:169
  75.5 5.6 %select_select_fusion = s32[1024]{0:T(1024)S(1)} fusion(pred[1024]{0:T(1024)(128)(4,1)S(1)} %get-tuple-element.79, pred[1024]{0:T(1024)(128)(4,1)S(1)} %get-tuple-element.78, pred[1024]{0:T(1024)(128)(4,1)S(1)} %get-tuple-element.77, pred[1024]{0:T(1024)(128)(4,1)S(1)} %get-tuple-element.76, pred[1024]{0:T(1024)(128)(4,1)S(1)} %get-tuple-element.75, ...), kind=kLoop, calls=%fused_computation.136 | loop fusion | flops 18432 | bytes 21572 | tf_op jit(solution)/shard_map/jit(_take)/select_n | solution.py:169
  81.3 0.7 slice_bitcast_fusion.4
  82.0 2.8 gather_fusion.1
  84.8 0.2 gather.23
  85.0 2.3 convert_reduce_fusion
  87.3 1.8 multiply_reduce_fusion
  89.1 0.9 copy-done.2
  90.0 6.4 %add_convert_fusion = bf16[16,64,3072]{2,1,0:T(8,128)(2,1)} fusion(bf16[16,64,3072]{2,1,0:T(8,128)(2,1)S(1)} %get-tuple-element.146, f32[16,3072]{1,0:T(8,128)S(1)} %get-tuple-element.121, f32[16,3072]{1,0:T(8,128)S(1)} %get-tuple-element.122, f32[16,64]{1,0:T(8,128)S(1)} %add_rsqrt_fusion.1, f32[16,64]{1,0:T(8,128)S(1)} %broadcast_multiply_fusion), kind=kLoop, calls=%fused_computation.21 | loop fusion | flops 18874368 | bytes 12984320 | tf_op jit(solution)/shard_map/convert_element_type | solution.py:159
  96.4 20.6 %convolution_convert_fusion.1 = bf16[1024,2304]{1,0:T(8,128)(2,1)} fusion(bf16[1024,3072]{1,0:T(8,128)(2,1)} %bitcast.126, bf16[3072,2304]{0,1:T(8,128)(2,1)} %bitcast.124), kind=kOutput, calls=%fused_computation.27 | convolution fusion | flops 14497873920 | bytes 25165824 | tf_op jit(solution)/shard_map/dot_general | solution.py:162
  117.1 6.6 %copy.38 = bf16[1024,2304]{0,1:T(8,128)(2,1)} copy(bf16[1024,2304]{1,0:T(8,128)(2,1)} %convolution_convert_fusion.1) | data formatting | bytes 9437184 | tf_op jit(solution)/shard_map/convert_element_type | solution.py:164
  123.7 4.8 %slice_bitcast_fusion = (bf16[1024,6,128]{0,2,1:T(8,128)(2,1)}, bf16[1024,6,128]{0,2,1:T(8,128)(2,1)}, bf16[1024,6,128]{0,2,1:T(8,128)(2,1)}) fusion(bf16[1024,3,6,128]{0,3,2,1:T(8,128)(2,1)} %bitcast.123), kind=kLoop, calls=%fused_computation.44 | loop fusion | bytes 9437184 | tf_op jit(solution)/shard_map/squeeze | solution.py:168
  128.5 1.9 copy.40
  130.4 2.6 copy.41
  133.0 69.6 %while.11 = (s32[]{:T(128)}, bf16[2,512,6,128]{3,1,2,0:T(8,128)(2,1)}, s32[2]{0:T(128)S(1)}, s32[1024]{0:T(1024)S(1)}, bf16[1024,6,128]{0,2,1:T(8,128)(2,1)}, /*...) while((s32[]{:T(128)}, ...), condition=%wide.region_20.21_spmd, body=%wide.region_17.20_spmd.sunk | while | flops 1636697088 | bytes 62425784 | solution.py:188
  133.0 0.7 dynamic_slice.66
  135.8 0.4 broadcast_compare_fusion.8
  136.1 7.8 %fusion.91 = f32[6,512,1024]{2,1,0:T(8,128)} fusion(bf16[1024,6,128]{2,0,1:T(8,128)(2,1)S(1)} %get-tuple-element.222, bf16[1024,6,128]{0,2,1:T(8,128)(2,1)} %get-tuple-element.221, s32[]{:T(128)S(6)} %select_n.324), kind=kOutput, calls=%fused_computation.16.clone.1 | convolution fusion | flops 805306368 | bytes 14942212 | tf_op jit(solution)/shard_map/while/body/eval_jaxpr/qhd,khd->hqk/dot_general | solution.py:175
  144.0 16.5 %fusion.92 = (f32[6,512]{1,0:T(8,128)S(1)}, f32[6,512,1024]{2,1,0:T(8,128)}) fusion(f32[6,512,1024]{2,1,0:T(8,128)} %fusion.91, pred[512,1024]{1,0:T(8,128)(4,1)S(1)} %broadcast_compare_fusion.8), kind=kOutput, calls=%fused_computation.170.clone.1 | output fusion | flops 18875392 | bytes 25702400 | tf_op jit(solution)/shard_map/while/body/eval_jaxpr/sub | solution.py:181
  160.5 7.4 %fusion.93 = bf16[2,512,6,128]{3,1,2,0:T(8,128)(2,1)} fusion(bf16[2,512,6,128]{3,1,2,0:T(8,128)(2,1)} %get-tuple-element.208, s32[]{:T(128)} %get-tuple-element.207, bf16[1024,6,128]{2,0,1:T(8,128)(2,1)S(1)} %copy-done.3, f32[6,512,1024]{2,1,0:T(8,128)} %get-tuple-element.195, f32[6,512]{1,0:T(8,128)S(1)} %get-tuple-element.196), kind=kOutput, calls=%fused_computation.14.clone.1 | convolution fusion | flops 811991040 | bytes 14955008 | tf_op jit(solution)/shard_map/while/body/eval_jaxpr/hqk,khd->qhd/dot_general | solution.py:183
  167.8 0.7 dynamic_slice.66
  170.6 0.4 broadcast_compare_fusion.8
  171.0 7.8 %fusion.91 = f32[6,512,1024]{2,1,0:T(8,128)} fusion(bf16[1024,6,128]{2,0,1:T(8,128)(2,1)S(1)} %get-tuple-element.222, bf16[1024,6,128]{0,2,1:T(8,128)(2,1)} %get-tuple-element.221, s32[]{:T(128)S(6)} %select_n.324), kind=kOutput, calls=%fused_computation.16.clone.1 | convolution fusion | flops 805306368 | bytes 14942212 | tf_op jit(solution)/shard_map/while/body/eval_jaxpr/qhd,khd->hqk/dot_general | solution.py:175
  178.8 16.5 %fusion.92 = (f32[6,512]{1,0:T(8,128)S(1)}, f32[6,512,1024]{2,1,0:T(8,128)}) fusion(f32[6,512,1024]{2,1,0:T(8,128)} %fusion.91, pred[512,1024]{1,0:T(8,128)(4,1)S(1)} %broadcast_compare_fusion.8), kind=kOutput, calls=%fused_computation.170.clone.1 | output fusion | flops 18875392 | bytes 25702400 | tf_op jit(solution)/shard_map/while/body/eval_jaxpr/sub | solution.py:181
  195.2 7.4 %fusion.93 = bf16[2,512,6,128]{3,1,2,0:T(8,128)(2,1)} fusion(bf16[2,512,6,128]{3,1,2,0:T(8,128)(2,1)} %get-tuple-element.208, s32[]{:T(128)} %get-tuple-element.207, bf16[1024,6,128]{2,0,1:T(8,128)(2,1)S(1)} %copy-done.3, f32[6,512,1024]{2,1,0:T(8,128)} %get-tuple-element.195, f32[6,512]{1,0:T(8,128)S(1)} %get-tuple-element.196), kind=kOutput, calls=%fused_computation.14.clone.1 | convolution fusion | flops 811991040 | bytes 14955008 | tf_op jit(solution)/shard_map/while/body/eval_jaxpr/hqk,khd->qhd/dot_general | solution.py:183
  202.6 2.5 copy.42
  205.1 2.7 reshape.498
  207.8 1.5 copy.43
  209.3 9.3 %convolution_convert_fusion = bf16[1024,3072]{1,0:T(8,128)(2,1)} fusion(bf16[1024,768]{1,0:T(8,128)(2,1)S(1)} %bitcast.128, bf16[768,3072]{1,0:T(8,128)(2,1)} %param.29), kind=kOutput, calls=%fused_computation.26 | convolution fusion | flops 4834983936 | bytes 12582912 | tf_op jit(solution)/shard_map/dot_general | solution.py:194
  218.6 9.1 %convert.13 = f32[16,4,16,3072]{3,2,1,0:T(8,128)} convert(bf16[16,4,16,3072]{3,2,1,0:T(8,128)(2,1)} %bitcast.122) | non-fusion elementwise | flops 3145728 | bytes 18874368 | tf_op jit(solution)/shard_map/reshape | solution.py:203
  227.7 56.7 %reduce-scatter.2.cloned.1.call-done = bf16[256,3072]{1,0:T(8,128)(2,1)} async-done(((bf16[1024,3072]{1,0:T(8,128)(2,1)}), bf16[256,3072]{1,0:T(8,128)(2,1)}) %reduce-scatter.2.cloned.1.call-update) | async-done | bytes 1572880 | tf_op jit(solution)/shard_map/reduce_scatter | solution.py:196
  284.5 4.3 %fusion.16 = bf16[16,1,16,3072]{3,2,1,0:T(8,128)(2,1)} fusion(bf16[16,1,16,3072]{3,2,1,0:T(8,128)(2,1)} %bitcast.129, f32[16,4,16,3072]{3,2,1,0:T(8,128)} %convert.13, s32[]{:T(128)S(6)} %select_n.241, f32[16,3072]{1,0:T(8,128)S(1)} %copy-done.4, pred[16]{0:T(512)(128)(4,1)S(1)} %copy-done.11), kind=kLoop, calls=%fused_computation.31 | loop fusion | flops 3932160 | bytes 6488084 | tf_op jit(solution)/shard_map/convert_element_type | solution.py:207
  (83 shorter events, 2.1 us)
Async XLA Ops:
  6.5 62.1 %copy-start = (f32[64,3,3072]{2,0,1:T(8,128)S(1)}, f32[64,3,3072]{2,0,1:T(8,128)}, u32[]{:S(2)}) copy-start(f32[64,3,3072]{2,0,1:T(8,128)} %param.27) | copy-start | bytes 7077892
  6.5 10.7 %copy-start.12 = (s32[64]{0:T(128)S(1)}, s32[64]{0:T(128)}, u32[]{:S(2)}) copy-start(s32[64]{0:T(128)} %param.25) | copy-start | bytes 772
  6.5 11.0 %copy-start.13 = (s32[64]{0:T(128)S(1)}, s32[64]{0:T(128)}, u32[]{:S(2)}) copy-start(s32[64]{0:T(128)} %param.26) | copy-start | bytes 772
  10.1 15.7 %copy-start.6 = (s32[8,128]{1,0:T(8,128)S(1)}, s32[8,128]{1,0:T(8,128)}, u32[]{:S(2)}) copy-start(s32[8,128]{1,0:T(8,128)} %constant.232.clone.1) | copy-start | bytes 12292
  10.8 16.4 %collective-permute-start = (bf16[1,2,32,512]{3,2,1,0:T(8,128)(2,1)}, bf16[1,2,32,512]{3,2,1,0:T(8,128)(2,1)}, u32[]{:S(2)}, u32[]{:S(2)}) collective-permute-start(bf16[1,2,32,512]{3,2,1,0:T(8,128)(2,1)} %get-tuple-element.119), channel_id=1, source_target_pairs={{0,4},{4,8},{8,12},{12,16},{16,20},{20,24},{24,28},{28,32},{32,36}... | collective-permute-start | bytes 196616 | tf_op jit(solution)/shard_map/ppermute | solution.py:22
  15.3 15.0 %collective-permute-start.1 = (bf16[1,2,32,512]{3,2,1,0:T(8,128)(2,1)S(1)}, bf16[1,2,32,512]{3,2,1,0:T(8,128)(2,1)}, u32[]{:S(2)}, u32[]{:S(2)}) collective-permute-start(bf16[1,2,32,512]{3,2,1,0:T(8,128)(2,1)S(1)} %get-tuple-element.118), channel_id=1, source_target_pairs={{4,0},{8,4},{12,8},{16,12},{20,16},{24,20},{28,24},{32,28},{36,32}... | collective-permute-start | bytes 196616 | tf_op jit(solution)/shard_map/ppermute | solution.py:23
  19.3 4.2 %copy-start.9 = (pred[16]{0:T(512)(128)(4,1)}, pred[16]{0:T(512)(128)(4,1)S(1)}, u32[]{:S(2)}) copy-start(pred[16]{0:T(512)(128)(4,1)S(1)} %get-tuple-element.128) | copy-start | bytes 52
  20.2 10.0 %copy-start.15 = (s32[8]{0:T(128)}, s32[8]{0:T(128)S(1)}, u32[]{:S(2)}) copy-start(s32[8]{0:T(128)S(1)} %iota_multiply_fusion) | copy-start | bytes 100
  38.4 11.3 %copy-start.8 = (pred[16,4]{1,0:T(8,128)(4,1)S(1)}, pred[16,4]{1,0:T(8,128)(4,1)}, u32[]{:S(2)}) copy-start(pred[16,4]{1,0:T(8,128)(4,1)} %compare_and_fusion) | copy-start | bytes 196
  38.4 43.6 %all-to-all-start = ((bf16[128,8,1024]{2,1,0:T(8,128)(2,1)}), bf16[128,8,1024]{2,1,0:T(8,128)(2,1)}, u32[]{:S(2)}, u32[]{:S(2)}) async-start(bf16[128,8,1024]{2,1,0:T(8,128)(2,1)} %bitcast.125), calls=%async_computation | async-start | bytes 4194304 | tf_op jit(solution)/shard_map/all_to_all | solution.py:142
  49.5 234.9 %reduce-scatter.2.cloned.1.call-start = ((), (), s32[]{:S(2)}) async-start(), calls=%async_computation.2 | async-start | bytes 7864320 | tf_op jit(solution)/shard_map/reduce_scatter | solution.py:196
  68.6 2.3 copy-start.5
  68.6 6.9 %copy-start.7 = (s32[8,128]{1,0:T(8,128)S(1)}, s32[8,128]{1,0:T(8,128)}, u32[]{:S(2)}) copy-start(s32[8,128]{1,0:T(8,128)} %constant.232.clone.1) | copy-start | bytes 12292
  68.6 6.9 %copy-start.16 = (s32[8]{0:T(128)S(1)}, s32[8]{0:T(128)}, u32[]{:S(2)}) copy-start(s32[8]{0:T(128)} %copy-done.15) | copy-start | bytes 100
  68.6 12.5 %copy-start.14 = (pred[16]{0:T(512)(128)(4,1)S(1)}, pred[16]{0:T(512)(128)(4,1)}, u32[]{:S(2)}) copy-start(pred[16]{0:T(512)(128)(4,1)} %get-tuple-element.101) | copy-start | bytes 52
  70.2 14.8 %copy-start.10 = (pred[16]{0:T(512)(128)(4,1)S(1)}, pred[16]{0:T(512)(128)(4,1)}, u32[]{:S(2)}) copy-start(pred[16]{0:T(512)(128)(4,1)} %copy-done.9) | copy-start | bytes 52
  70.2 14.8 %copy-start.17 = (bf16[64,3072]{1,0:T(8,128)(2,1)S(1)}, bf16[64,3072]{1,0:T(8,128)(2,1)}, u32[]{:S(2)}) copy-start(bf16[64,3072]{1,0:T(8,128)(2,1)} %param.23) | copy-start | bytes 1179652
  70.2 14.8 %copy-start.18 = (f32[3072]{0:T(1024)S(1)}, f32[3072]{0:T(1024)}, u32[]{:S(2)}) copy-start(f32[3072]{0:T(1024)} %param.24) | copy-start | bytes 36868
  87.3 2.7 copy-start.2
  144.0 16.5 %copy-start.3 = (bf16[1024,6,128]{2,0,1:T(8,128)(2,1)S(1)}, bf16[1024,6,128]{2,0,1:T(8,128)(2,1)}, u32[]{:S(2)}) copy-start(bf16[1024,6,128]{2,0,1:T(8,128)(2,1)} %get-tuple-element.223) | copy-start | bytes 4718596 | tf_op jit(solution)/shard_map/while
  178.8 16.5 %copy-start.3 = (bf16[1024,6,128]{2,0,1:T(8,128)(2,1)S(1)}, bf16[1024,6,128]{2,0,1:T(8,128)(2,1)}, u32[]{:S(2)}) copy-start(bf16[1024,6,128]{2,0,1:T(8,128)(2,1)} %get-tuple-element.223) | copy-start | bytes 4718596 | tf_op jit(solution)/shard_map/while
  218.6 65.9 %copy-start.4 = (f32[16,3072]{1,0:T(8,128)S(1)}, f32[16,3072]{1,0:T(8,128)}, u32[]{:S(2)}) copy-start(f32[16,3072]{1,0:T(8,128)} %get-tuple-element.120) | copy-start | bytes 589828
  218.6 65.8 %copy-start.11 = (pred[16]{0:T(512)(128)(4,1)S(1)}, pred[16]{0:T(512)(128)(4,1)}, u32[]{:S(2)}) copy-start(pred[16]{0:T(512)(128)(4,1)} %copy-done.9) | copy-start | bytes 52
  284.5 4.3 %copy-start.1 = (f32[64,3,3072]{2,0,1:T(8,128)S(1)}, f32[64,3,3072]{2,0,1:T(8,128)}, u32[]{:S(2)}) copy-start(f32[64,3,3072]{2,0,1:T(8,128)} %param.27) | copy-start | bytes 7077892
Sparse Core Ops, SparseCore 0:
  218.7 65.6 reduce-scatter.1
where the time goes:
time: 297 us; the launch traced here: 296 us
  other arithmetic  75.7 us (25%)
  matrix products  72.9 us (25%)
  waiting for transfers between devices  56.7 us (19%)
  local copies, waits for them, and re-layouts  54.4 us (18%)
  starting transfers between devices  17.7 us (6%)
  between operations  13.8 us (5%)
  loops' own time  4.17 us (1%)
    reduce_scatter x1, waiting for transfers between devices, shards(): lax.psum_scatter(term(jnp.int32(0), lax.axis_size('seq') * (fr_slab * tok...  56.7 us
    sub x2, other arithmetic, one_block(): weights = jnp.exp(masked - top)  32.9 us
    dot_general x1, matrix products, shards(): jnp.dot(hidden, w_qkv.reshape(model, 3 * head_width), preferred_element_t...  20.6 us
    unnamed x37, local copies, waits for them, and re-layouts  19.6 us
    dot_general x2, matrix products, one_block(): jnp.einsum('qhd,khd->hqk', query, keys, preferred_element_type=jnp.float32)  15.6 us
    dot_general x2, matrix products, one_block(): jnp.einsum('hqk,khd->qhd', probs, vals, preferred_element_type=jnp.float32)  14.7 us
    all_to_all x1, starting transfers between devices, shards(): lax.all_to_all(wide, ('clip', 'seq'), split_axis=0, concat_axis=0, tiled=...  11.1 us
    dot_general x1, matrix products, term(): return jnp.dot(piece, w_out, preferred_element_type=jnp.float32)  9.26 us
  transfers between devices with their start and end apart: 4, of which 1 were waited for; matrix products, arithmetic and copies ran while one was open for 18% of the time, Pallas kernels for 0%

commit v1 on v0

v1 whole, which is shorter than its diff:
```python
import functools

import jax
import jax.numpy as jnp
from jax import lax
from jax.experimental import pallas as pl
from jax.experimental.pallas import tpu as pltpu
from jax.sharding import PartitionSpec as P

MESH = pl.DeviceIdType.MESH
F32 = jnp.float32
BF16 = jnp.bfloat16
D = 3072
QC = 768
LOG2E = 1.4426950408889634


def mm(a, b):
    return jnp.dot(a, b, preferred_element_type=F32)


def mm_t(a, b):
    return lax.dot_general(a, b, (((1,), (1,)), ((), ())), preferred_element_type=F32)


def iota(shape, dim):
    return lax.broadcasted_iota(jnp.int32, shape, dim)


def body(
    vae,
    gain,
    w_conv,
    b_conv,
    w_lat,
    b_lat,
    w_emb,
    b_emb,
    lengths,
    owner,
    mods,
    w_qkv,
    w_out,
    out,
    xin,
    act,
    wconv,
    ym,
    wemb,
    modv,
    wq,
    lhs,
    mqk,
    wown,
    wbuf,
    pbuf,
    precv,
    pk,
    mb,
    keysp,
    attn_int,
    attn_own,
    attn_blk,
    acc,
    ptf,
    loc_sem,
    halo_s,
    halo_r,
    zs_s,
    zs_r,
    p1_s,
    p1_r,
    p2_s,
    p2_r,
    fw_s,
    fw_r,
    sib_s,
    sib_r,
    aa_s,
    aa_r,
    mb_s,
    mb_r,
    pk_s,
    pk_r,
):
    c = lax.axis_index("clip")
    z = lax.axis_index("seq")
    core = lax.rem(c, 2)
    x = lax.rem(lax.div(c, 2), 4)
    y = lax.div(c, 8)

    def in_plane(dx, dy):
        return (lax.rem(y + dy + 4, 4) * 8 + lax.rem(x + dx + 4, 4) * 2 + core, z)

    sibling = (c + 1 - 2 * core, z)

    def remote(src, dst, ss, rs, dev):
        return pltpu.make_async_remote_copy(
            src_ref=src, dst_ref=dst, send_sem=ss, recv_sem=rs, device_id=dev, device_id_type=MESH
        )

    loads = {}

    def load(name, src, dst, k):
        loads[name] = pltpu.make_async_copy(src, dst, loc_sem.at[k])
        loads[name].start()

    load("vae", vae, xin.at[pl.ds(1, 16)], 0)
    load("wconv", w_conv, wconv, 1)
    load("wemb", w_emb, wemb, 2)
    load("mods", mods, modv, 3)
    for j in range(3):
        load(("wq", j), w_qkv.at[j], wq.at[j], 4 + j)
    for q in range(4):
        load(("wo", q), w_out.at[:, pl.ds(q * QC, QC)], wown.at[q], 7 + q)

    barrier = pltpu.get_barrier_semaphore()

    def greet(g, carry):
        @pl.when(g != c)
        def _():
            pl.semaphore_signal(barrier, inc=1, device_id=(g, z), device_id_type=MESH)

        return carry

    lax.fori_loop(0, 32, greet, 0)
    for r in range(1, 4):
        pl.semaphore_signal(
            barrier, inc=1, device_id=(c, lax.rem(z + r, 4)), device_id_type=MESH
        )
    pl.semaphore_wait(barrier, 34)

    nxt = (lax.rem(c + 1, 32), z)
    prv = (lax.rem(c + 31, 32), z)
    halo = [
        remote(vae.at[pl.ds(15, 1)], xin.at[pl.ds(0, 1)], halo_s.at[0], halo_r.at[0], nxt),
        remote(vae.at[pl.ds(0, 1)], xin.at[pl.ds(17, 1)], halo_s.at[1], halo_r.at[1], prv),
    ]
    for cp in halo:
        cp.start()

    quarter = [2 * core, 2 * core + 1]
    piece = [
        pl.multiple_of(y * 192 + x * 48, 16),
        pl.multiple_of(x * 192 + y * 48, 16),
    ]
    scatter = []
    for k in range(2):
        for r in range(1, 4):
            i = k * 3 + r - 1
            cp = remote(
                w_out.at[pl.ds(piece[k], 48), pl.ds(pl.multiple_of(quarter[k] * QC, QC), QC)],
                wbuf.at[r, quarter[k], pl.ds(piece[k], 48), :],
                zs_s.at[i],
                zs_r.at[i],
                (c, lax.rem(z - r + 4, 4)),
            )
            cp.start()
            scatter.append(cp)

    lane = iota((8, 128), 1)
    fzero = jnp.zeros((8, 128), jnp.int32)

    def table(i, carry):
        starts, lens, owners, total, p_own, s_a, s_b, l_a, l_b = carry
        n = lengths[i]
        o = owner[i]
        here = lane == i
        starts = jnp.where(here, total, starts)
        lens = jnp.where(here, n, lens)
        owners = jnp.where(here, o, owners)
        mine = (o == c).astype(jnp.int32)
        low = (i < 32).astype(jnp.int32)
        p_own = p_own + mine * low * i
        s_a = s_a + mine * low * total
        s_b = s_b + mine * (1 - low) * total
        l_a = l_a + mine * low * n
        l_b = l_b + mine * (1 - low) * n
        return starts, lens, owners, total + n, p_own, s_a, s_b, l_a, l_b

    i0 = jnp.int32(0)
    starts, lens, owners, total, p_own, s_a, s_b, l_a, l_b = lax.fori_loop(
        0, 64, table, (fzero - 1, fzero, fzero - 1, i0, i0, i0, i0, i0, i0)
    )
    starts = jnp.where(lane == 64, total, starts)
    p_own = jnp.minimum(p_own, 31)

    def activate(v):
        v = v.astype(F32)
        power = jnp.mean(v * v, axis=-1, keepdims=True)
        t = v * lax.rsqrt(power + 1e-06) * gain[...]
        return (t / (1.0 + jnp.exp(-t))).astype(BF16)

    loads["vae"].wait()

    def act_step(i, carry):
        act[pl.ds(1 + 2 * i, 2)] = activate(xin[pl.ds(1 + 2 * i, 2)])
        return carry

    lax.fori_loop(0, 8, act_step, 0)

    for cp in scatter:
        cp.wait_recv()
    phase1 = []
    for k in range(2):
        for n, d in enumerate((1, -1, 2)):
            i = k * 3 + n
            region = wbuf.at[pl.ds(1, 3), quarter[k], pl.ds(piece[k], 48), :]
            dev = in_plane(d, 0) if k == 0 else in_plane(0, d)
            cp = remote(region, region, p1_s.at[i], p1_r.at[i], dev)
            cp.start()
            phase1.append(cp)

    def wait_phase1():
        for k in range(2):
            for n, d in enumerate((1, -1, 2)):
                i = k * 3 + n
                if k == 0:
                    row = y * 192 + lax.rem(x - d + 4, 4) * 48
                else:
                    row = x * 192 + lax.rem(y - d + 4, 4) * 48
                region = wbuf.at[
                    pl.ds(1, 3), quarter[k], pl.ds(pl.multiple_of(row, 16), 48), :
                ]
                remote(region, region, p1_s.at[i], p1_r.at[i], sibling).wait_recv()

    for cp in halo:
        cp.wait_recv()
    act[pl.ds(0, 1)] = activate(xin[pl.ds(0, 1)])
    act[pl.ds(17, 1)] = activate(xin[pl.ds(17, 1)])

    loads["wconv"].wait()
    fid = c * 16 + iota((16, 128), 0)
    starts16 = jnp.concatenate([starts, starts], axis=0)
    lane16 = iota((16, 128), 1)
    begins = jnp.max(
        jnp.where((starts16 == fid) & (lane16 <= 64), 1.0, 0.0), axis=1, keepdims=True
    )
    ends = jnp.max(
        jnp.where((starts16 == fid + 1) & (lane16 <= 64), 1.0, 0.0), axis=1, keepdims=True
    )
    keep0 = jnp.broadcast_to(1.0 - begins, (16, 128))
    keep2 = jnp.broadcast_to(1.0 - ends, (16, 128))
    lat8 = jnp.concatenate([w_lat[...]] * 8, axis=0)
    blat8 = jnp.concatenate([b_lat[...]] * 8, axis=1)
    pos = iota((256, 128), 0)
    ln = iota((256, 128), 1)
    pos_key = ((pos & 31) >> 4) * 4 + ((pos >> 5) & 1) * 2 + (pos & 1)
    place_mask = pos_key == (ln >> 4)
    for i in range(4):
        f0 = 4 * i
        left = act[pl.ds(f0, 4)].reshape(256, 512)
        mid = act[pl.ds(f0 + 1, 4)].reshape(256, 512)
        right = act[pl.ds(f0 + 2, 4)].reshape(256, 512)

        def rows_of(col):
            return jnp.concatenate(
                [
                    jnp.broadcast_to(col[f0 + f : f0 + f + 1, 0:1], (64, 512))
                    for f in range(4)
                ],
                axis=0,
            )

        conv = b_conv[...] + mm(mid, wconv[1])
        conv = conv + rows_of(keep0) * mm(left, wconv[0])
        conv = conv + rows_of(keep2) * mm(right, wconv[2])
        resid = (xin[pl.ds(f0 + 1, 4)].reshape(256, 512).astype(F32) + conv).astype(BF16)
        lat = mm_t(resid, lat8) + blat8
        ym[pl.ds(256 * i, 256), :] = jnp.where(place_mask, lat, 0.0).astype(BF16)

    srow = iota((128, 1024), 0)
    scol = iota((128, 1024), 1)
    pick_pos = ((srow & 15) == (scol >> 6)) & ((srow >> 4) == ((scol >> 1) & 7))
    patches = mm(pick_pos.astype(F32).astype(BF16), ym[...])
    frame_rows = jnp.concatenate([patches[16 * j : 16 * j + 16] for j in range(8)], axis=1)
    halves = jnp.concatenate([frame_rows[:, :512], frame_rows[:, 512:]], axis=0).astype(BF16)

    def column(vec, sel):
        return jnp.sum(jnp.where(sel, vec, 0), axis=1, keepdims=True)

    g_row = iota((512, 128), 0) >> 4
    g_lane = iota((512, 128), 1)
    own512 = jnp.broadcast_to(owners[0:1], (512, 128)) == g_row
    st512 = jnp.broadcast_to(starts[0:1], (512, 128))
    ln512 = jnp.broadcast_to(lens[0:1], (512, 128))
    sel_a = own512 & (g_lane < 32)
    sel_b = own512 & (g_lane >= 32) & (g_lane < 64)
    ga_s, ga_l = column(st512, sel_a), column(ln512, sel_a)
    gb_s, gb_l = column(st512, sel_b), column(ln512, sel_b)
    prow = iota((512, 32), 0)
    pcol = iota((512, 32), 1)
    frame = c * 16 + (pcol & 15)
    at = prow & 7
    wanted = ((frame == ga_s + at) & (at < ga_l)) | ((frame == gb_s + at) & (at < gb_l))
    wanted = wanted & (((prow >> 3) & 1) == (pcol >> 4))
    pbuf[...] = mm(wanted.astype(F32).astype(BF16), halves).astype(BF16).reshape(32, 16, 512)

    def send_rows(g, carry):
        @pl.when(g != c)
        def _():
            remote(pbuf.at[g], precv.at[c], aa_s.at[g], aa_r.at[c], (g, z)).start()

        return carry

    lax.fori_loop(0, 32, send_rows, 0)
    precv[c] = pbuf[c]

    loads["wemb"].wait()
    loads["mods"].wait()
    we = wemb[...].astype(F32)
    we = we - jnp.mean(we, axis=1, keepdims=True)
    be = b_emb[...]
    be = be - jnp.mean(be, axis=1, keepdims=True)
    scale_a = 1.0 + modv[1, pl.ds(p_own, 1), :]
    scale_b = 1.0 + modv[1, pl.ds(p_own + 32, 1), :]
    shift_a = modv[0, pl.ds(p_own, 1), :]
    shift_b = modv[0, pl.ds(p_own + 32, 1), :]
    lhs[0:64] = (we * scale_a).astype(BF16)
    lhs[64:128] = (we * scale_b).astype(BF16)
    extra = jnp.concatenate(
        [be * scale_a, shift_a, be * scale_b, shift_b, jnp.zeros((12, D), F32)], axis=0
    )
    lhs[128:144] = extra.astype(BF16)
    full = jnp.concatenate([we, be, jnp.zeros((63, D), F32)], axis=0)
    hi = full.astype(BF16)
    lo = (full - hi.astype(F32)).astype(BF16)
    gram = (mm_t(hi, hi) + mm_t(hi, lo) + mm_t(lo, hi)) * (1.0 / D)
    gram_hi = gram.astype(BF16)
    gram_lo = (gram - gram_hi.astype(F32)).astype(BF16)

    bias_row = iota((80, 128), 0)
    bias_col = iota((80, 128), 1)
    for j in range(3):
        loads[("wq", j)].wait()
        prod = mm(lhs[...], wq[j]).astype(BF16)
        for k in range(2):
            part = jnp.concatenate([prod[64 * k : 64 * k + 64], prod[128:144]], axis=0)
            if j < 2:
                mqk[j, k] = part
            else:
                mb[0, k, 1, 0:80, :] = part
    for k in range(2):
        one = jnp.where((bias_row == 65 + 2 * k) & (bias_col == 68), 1.0, 0.0)
        for h in range(6):
            mq = mqk[0, k, :, 128 * h : 128 * h + 128]
            mk = jnp.concatenate(
                [mqk[1, k, :, 128 * h : 128 * h + 128], jnp.zeros((48, 128), BF16)], axis=0
            )
            bil = mm_t(mq, mk) * (LOG2E * 128 ** (-0.5)) + one
            mb[0, k, 0, 0:80, 128 * h : 128 * h + 128] = bil.astype(BF16)
    zero_rows = jnp.zeros((48, QC), BF16)
    for r in range(4):
        for k in range(2):
            for j in range(2):
                mb[r, k, j, 80:128, :] = zero_rows
    mb_send = []
    for r in range(1, 4):
        cp = remote(
            mb.at[0, :, :, pl.ds(0, 80), :],
            mb.at[r, :, :, pl.ds(0, 80), :],
            mb_s.at[r - 1],
            mb_r.at[r - 1],
            (c, lax.rem(z - r + 4, 4)),
        )
        cp.start()
        mb_send.append(cp)

    wait_phase1()
    line = [y, x]

    def block(k, d, half=None):
        row = lax.rem(line[k] + d + 4, 4) * 192
        size = 192
        if half is not None:
            row = row + half * 96
            size = 96
        return (pl.ds(1, 3), quarter[k], pl.ds(pl.multiple_of(row, 16), size), slice(None))

    def along(k, d):
        return in_plane(0, d) if k == 0 else in_plane(d, 0)

    sends = []

    def push(region, ss, rs, dev):
        cp = remote(wbuf.at[region], wbuf.at[region], ss, rs, dev)
        cp.start()
        sends.append(cp)

    def arrived(region, ss, rs):
        remote(wbuf.at[region], wbuf.at[region], ss, rs, sibling).wait_recv()

    for k in range(2):
        for n, d in enumerate((1, -1)):
            push(block(k, 0), p2_s.at[2 * k + n], p2_r.at[2 * k + n], along(k, d))
    for k in range(2):
        push(block(k, 0), sib_s.at[4 * k], sib_r.at[4 * k], sibling)

    def get_rows(s, carry):
        @pl.when(s != c)
        def _():
            remote(pbuf.at[s], precv.at[s], aa_s.at[s], aa_r.at[s], (s, z)).wait_recv()

        return carry

    lax.fori_loop(0, 32, get_rows, 0)
    krow = iota((32, 512), 0)
    kcol = iota((32, 512), 1)
    kj = krow & 7
    k_first = jnp.where(((krow >> 3) & 1) == 0, s_a, s_b)
    k_len = jnp.where(((krow >> 3) & 1) == 0, l_a, l_b)
    take = (
        (((k_first + kj) >> 4) == (kcol >> 4))
        & (kj == (kcol & 7))
        & ((krow >> 4) == ((kcol >> 3) & 1))
        & (kj < k_len)
    )
    pk[0] = mm(take.astype(F32).astype(BF16), precv[...].reshape(512, 512)).astype(BF16)
    pk_send = []
    for r in range(1, 4):
        cp = remote(
            pk.at[0], pk.at[r], pk_s.at[r - 1], pk_r.at[r - 1], (c, lax.rem(z - r + 4, 4))
        )
        cp.start()
        pk_send.append(cp)
    for cp in pk_send:
        cp.wait_recv()

    klane = iota((512, 128), 1)
    kpos = iota((512, 128), 0) & 7
    tokens = []
    for k in range(2):
        blocks = []
        for r in range(4):
            rows = pk[r].astype(F32)
            for half in range(2):
                for b in range(8):
                    lo_row = half * 16 + 8 * k
                    blocks.append(rows[lo_row : lo_row + 8, 64 * b : 64 * b + 64])
        pt = jnp.concatenate(blocks, axis=0)
        pt = jnp.concatenate([pt, jnp.zeros((512, 64), F32)], axis=1)
        tokens.append(pt[0:128].astype(BF16))
        aug = jnp.where(klane == 64, 1.0, pt)
        augb = aug.astype(BF16)
        quad = mm(augb, gram_hi) + mm(augb, gram_lo)
        var = jnp.sum(aug * quad, axis=1, keepdims=True)
        rstd = lax.rsqrt(jnp.maximum(var, 0.0) + 1e-06)
        length = l_a if k == 0 else l_b
        bias = jnp.where(kpos < length, 0.0, -1e30)
        full_row = pt * rstd
        full_row = jnp.where(klane == 64 + 2 * k, rstd, full_row)
        full_row = jnp.where(klane == 65 + 2 * k, 1.0, full_row)
        full_row = jnp.where(klane == 68, bias, full_row)
        keysp[k] = full_row.astype(BF16)

    trow = iota((256, 256), 0)
    tcol = iota((256, 256), 1)
    tj = tcol & 7
    second = tcol >> 7
    t_slot = jnp.where(second == 0, tj, tj + l_a)
    t_ok = tj < jnp.where(second == 0, l_a, l_b)
    t_patch = ((tcol >> 3) & 1) * 8 + ((tcol >> 4) & 7)
    perm = ((trow >> 4) == t_slot) & ((trow & 15) == t_patch) & t_ok
    perm = perm.astype(F32).astype(BF16)
    ptf[...] = mm(perm, jnp.concatenate(tokens, axis=0)).astype(BF16)

    def attend(r):
        def one_clip(k, carry):
            keys = keysp[k]
            queries = mm(keys[0:128], mb[r, k, 0]).astype(BF16)
            den_lane = 65 + 2 * k
            sel = iota((128, 128), 1) == den_lane
            for h in range(6):
                s = mm_t(queries[:, 128 * h : 128 * h + 128], keys)
                top = jnp.max(s, axis=1, keepdims=True)
                w = jnp.exp2(s - top).astype(BF16)
                rr = mm(w, keys)
                den = jnp.sum(jnp.where(sel, rr, 0.0), axis=1, keepdims=True)
                rn = (rr / den).astype(BF16)
                o = mm(rn, mb[r, k, 1, :, 128 * h : 128 * h + 128])
                attn_int[pl.ds(pl.multiple_of(128 * k, 128), 128), 128 * h : 128 * h + 128] = (
                    o.astype(BF16)
                )
            return carry

        lax.fori_loop(0, 2, one_clip, 0)
        return mm(perm, attn_int[...]).astype(BF16)

    attn_own[...] = attend(0)

    for k in range(2):
        for n, d in enumerate((1, -1)):
            arrived(block(k, -d), p2_s.at[2 * k + n], p2_r.at[2 * k + n])
            push(block(k, -d, n), fw_s.at[2 * k + n], fw_r.at[2 * k + n], along(k, d))
    for k in range(2):
        for n, d in enumerate((1, -1)):
            push(block(k, -d), sib_s.at[4 * k + 1 + n], sib_r.at[4 * k + 1 + n], sibling)

    for q in range(4):
        loads[("wo", q)].wait()
        acc[q] = mm(attn_own[...], wown[q])

    def foreign(r, carry):
        remote(
            mb.at[0, :, :, pl.ds(0, 80), :],
            mb.at[r, :, :, pl.ds(0, 80), :],
            mb_s.at[r - 1],
            mb_r.at[r - 1],
            sibling,
        ).wait_recv()
        at_r = attend(r)
        for b in range(4):
            attn_blk[r - 1, b] = at_r[:, 192 * b : 192 * b + 192]
        return carry

    lax.fori_loop(1, 4, foreign, 0)

    def project(q, blk):
        rows = pl.ds(pl.multiple_of(blk * 192, 16), 192)
        total = acc[q]
        for r in range(3):
            total = total + mm(attn_blk[r, blk], wbuf[r + 1, q, rows, :])
        acc[q] = total

    other = [2 - 2 * core, 3 - 2 * core]

    def from_sibling(k, d, i):
        row = lax.rem(line[k] + d + 4, 4) * 192
        region = (pl.ds(1, 3), other[k], pl.ds(pl.multiple_of(row, 16), 192), slice(None))
        arrived(region, sib_s.at[4 * k + i], sib_r.at[4 * k + i])

    def project_step(k, d, i):
        blk = lax.rem(line[k] + d + 4, 4)
        project(quarter[k], blk)
        from_sibling(k, d, i)
        project(other[k], blk)

    for k in range(2):
        project_step(k, 0, 0)
    for k in range(2):
        for n, d in enumerate((1, -1)):
            project_step(k, -d, 1 + n)
    for k in range(2):
        for n, d in enumerate((1, -1)):
            arrived(block(k, 2, n), fw_s.at[2 * k + n], fw_r.at[2 * k + n])
        push(block(k, 2), sib_s.at[4 * k + 3], sib_r.at[4 * k + 3], sibling)
    for k in range(2):
        project_step(k, 2, 3)

    orow = iota((256, QC), 0) >> 4
    in_a = orow < l_a
    live = orow < l_a + l_b
    for q in range(4):
        cols = slice(q * QC, q * QC + QC)
        res = mm(ptf[:, 0:64], wemb[:, cols]) + b_emb[:, cols]
        gate = jnp.where(
            in_a, modv[2, pl.ds(p_own, 1), cols], modv[2, pl.ds(p_own + 32, 1), cols]
        )
        out[:, cols] = jnp.where(live, res + gate * acc[q], 0.0).astype(BF16)

    for cp in halo + scatter + phase1 + mb_send + pk_send + sends:
        cp.wait_send()

    def done_rows(g, carry):
        @pl.when(g != c)
        def _():
            remote(pbuf.at[g], precv.at[c], aa_s.at[g], aa_r.at[c], (g, z)).wait_send()

        return carry

    lax.fori_loop(0, 32, done_rows, 0)


def shards(
    vae_in,
    vae_gain,
    w_conv,
    b_conv,
    w_lat,
    b_lat,
    w_emb,
    b_emb,
    clip_lengths,
    clip_owner,
    clip_mod,
    w_qkv,
    w_out,
):
    anyspec = pl.BlockSpec(memory_space=pl.ANY)
    vmem = pl.BlockSpec(memory_space=pltpu.VMEM)
    smem = pl.BlockSpec(memory_space=pltpu.SMEM)
    dma = pltpu.SemaphoreType.DMA
    out = pl.pallas_call(
        body,
        out_shape=jax.ShapeDtypeStruct((256, D), BF16),
        in_specs=[
            anyspec,
            vmem,
            anyspec,
            vmem,
            vmem,
            vmem,
            anyspec,
            vmem,
            smem,
            smem,
            anyspec,
            anyspec,
            anyspec,
        ],
        out_specs=vmem,
        scratch_shapes=[
            pltpu.VMEM((18, 64, 512), BF16),
            pltpu.VMEM((18, 64, 512), BF16),
            pltpu.VMEM((3, 512, 512), BF16),
            pltpu.VMEM((1024, 128), BF16),
            pltpu.VMEM((64, D), BF16),
            pltpu.VMEM((3, 64, D), F32),
            pltpu.VMEM((3, D, QC), BF16),
            pltpu.VMEM((144, D), BF16),
            pltpu.VMEM((2, 2, 80, QC), BF16),
            pltpu.VMEM((4, QC, QC), BF16),
            pltpu.VMEM((4, 4, QC, QC), BF16),
            pltpu.VMEM((32, 16, 512), BF16),
            pltpu.VMEM((32, 16, 512), BF16),
            pltpu.VMEM((4, 32, 512), BF16),
            pltpu.VMEM((4, 2, 2, 128, QC), BF16),
            pltpu.VMEM((2, 512, 128), BF16),
            pltpu.VMEM((256, QC), BF16),
            pltpu.VMEM((256, QC), BF16),
            pltpu.VMEM((3, 4, 256, 192), BF16),
            pltpu.VMEM((4, 256, QC), F32),
            pltpu.VMEM((256, 128), BF16),
            dma((11,)),
            dma((2,)),
            dma((2,)),
            dma((6,)),
            dma((6,)),
            dma((6,)),
            dma((6,)),
            dma((4,)),
            dma((4,)),
            dma((4,)),
            dma((4,)),
            dma((8,)),
            dma((8,)),
            dma((32,)),
            dma((32,)),
            dma((3,)),
            dma((3,)),
            dma((3,)),
            dma((3,)),
        ],
        compiler_params=pltpu.CompilerParams(
            collective_id=0, has_side_effects=True, vmem_limit_bytes=60 * 2**20
        ),
    )(
        vae_in.reshape(16, 64, 512),
        vae_gain.reshape(1, 512),
        w_conv,
        b_conv.reshape(1, 512),
        w_lat.T,
        b_lat.reshape(1, 16),
        w_emb,
        b_emb.reshape(1, D),
        clip_lengths,
        clip_owner,
        clip_mod.transpose(1, 0, 2),
        w_qkv.transpose(1, 0, 2),
        w_out,
    )
    return out.reshape(16, 1, 16, D)


def solution(mesh):
    in_specs = (
        P("clip", "seq", None, None),
        P(),
        P(),
        P(),
        P(),
        P(),
        P(),
        P(),
        P(),
        P(),
        P(),
        P(None, None, "seq"),
        P("seq", None),
    )
    out_specs = P("clip", "seq", None, None)
    return jax.shard_map(shards, mesh=mesh, in_specs=in_specs, out_specs=out_specs, check_vma=False)
```

time: 297 us -> 96.4 us (0.32)
  Pallas kernels: 0 us -> 93.6 us
  other arithmetic: 75.7 us -> 0 us
  matrix products: 72.9 us -> 0 us
  waiting for transfers between devices: 56.7 us -> 0 us
  local copies, waits for them, and re-layouts: 54.4 us -> 2.69 us
  starting transfers between devices: 17.7 us -> 0 us
  between operations: 13.8 us -> 0.01 us
  loops' own time: 4.17 us -> 0 us
    pallas_call x0 -> x1, Pallas kernels: none -> 93.6 us  [shards(): pl.pallas_call(body, out_shape=jax.ShapeDtypeStruct((256, D), BF16), in_s...]
    dot_general x10 -> x0, matrix products: 72.9 us -> none  [the longest x1 20.6 us: shards(): jnp.dot(hidden, w_qkv.reshape(model, 3 * head_width), preferred_element_t...]
    reduce_scatter x1 -> x0, waiting for transfers between devices: 56.7 us -> none  [shards(): lax.psum_scatter(term(jnp.int32(0), lax.axis_size('seq') * (fr_slab * tok...]
    sub x7 -> x0, other arithmetic: 33.7 us -> none  [the longest x2 32.9 us: one_block(): weights = jnp.exp(masked - top)]
    unnamed x37 -> x1, local copies, waits for them, and re-layouts: 19.6 us -> 2.69 us
    convert_element_type x3 -> x0, other arithmetic: 12.6 us -> none  [the longest x1 6.45 us: shards(): hidden = hidden.astype(jnp.bfloat16).reshape(tokg, model)]
    all_to_all x1 -> x0, starting transfers between devices: 11.1 us -> none  [shards(): lax.all_to_all(wide, ('clip', 'seq'), split_axis=0, concat_axis=0, tiled=...]
    reshape x1 -> x0, other arithmetic: 9.11 us -> none  [shards(): token_values.reshape(fr_slab, regions, tok_frame, model)]
  transfers between devices with their start and end apart: 4 -> 0, of which waited for: 1 -> 0; matrix products, arithmetic and copies ran while one was open for 18% -> 0% of each run, Pallas kernels for 0% -> 0%
where the time goes in v1:
time: 96.4 us; the launch traced here: 96.3 us
  Pallas kernels  93.6 us (97%)
  local copies, waits for them, and re-layouts  2.69 us (3%)
    pallas_call x1, Pallas kernels, shards(): pl.pallas_call(body, out_shape=jax.ShapeDtypeStruct((256, D), BF16), in_s...  93.6 us
    unnamed x1, local copies, waits for them, and re-layouts  2.69 us

profile of v1, /device:TPU:1, one launch (start us, length us, event | category | flops | bytes accessed | tf_op | source)
XLA Modules:
  0.0 96.3 jit_solution(3349803063192601651)
XLA Ops:
  0.0 93.6 %shard_map.127 = bf16[256,3072]{1,0:T(8,128)(2,1)} custom-call(bf16[16,64,512]{2,1,0:T(8,128)(2,1)} %bitcast.14, f32[1,512]{1,0:T(1,128)} %bitcast.17, bf16[3,512,512]{2,1,0:T(8,128)(2,1)} %w_conv.1, f32[1,512]{1,0:T(1,128)} %bitcast.18, bf16[16,512]{1,0:T(8,128)(2,1)} %bitcast.15, f32[1,16]{1,0:T(1,128)} %bitcast.19, bf16[64,3072]{1,0:T(8,128)(2,1)} %w_emb.1, ...), custom_call_target="tpu_custom_call" | custom-call | tf_op jit(solution)/shard_map/pallas_call | solution.py:593
  93.6 2.7 %copy.16 = bf16[16,1,16,3072]{3,2,1,0:T(8,128)(2,1)} copy(bf16[16,1,16,3072]{3,2,1,0:T(8,128)(2,1)} %bitcast.12) | data formatting | bytes 3145728

commit v2 on v1

--- a/solution.py
+++ b/solution.py
@@ -58,6 +58,7 @@
     pk,
     mb,
     keysp,
+    keyst,
     attn_int,
     attn_own,
     attn_blk,
@@ -68,12 +69,16 @@
     halo_r,
     zs_s,
     zs_r,
-    p1_s,
-    p1_r,
-    p2_s,
-    p2_r,
-    fw_s,
-    fw_r,
+    zf_s,
+    zf_r,
+    ra_s,
+    ra_r,
+    rb_s,
+    rb_r,
+    fa_s,
+    fa_r,
+    fb_s,
+    fb_r,
     sib_s,
     sib_r,
     aa_s,
@@ -140,23 +145,127 @@
         cp.start()
 
     quarter = [2 * core, 2 * core + 1]
-    piece = [
-        pl.multiple_of(y * 192 + x * 48, 16),
-        pl.multiple_of(x * 192 + y * 48, 16),
-    ]
-    scatter = []
-    for k in range(2):
-        for r in range(1, 4):
-            i = k * 3 + r - 1
-            cp = remote(
-                w_out.at[pl.ds(piece[k], 48), pl.ds(pl.multiple_of(quarter[k] * QC, QC), QC)],
-                wbuf.at[r, quarter[k], pl.ds(piece[k], 48), :],
-                zs_s.at[i],
-                zs_r.at[i],
-                (c, lax.rem(z - r + 4, 4)),
-            )
-            cp.start()
-            scatter.append(cp)
+    other = [2 - 2 * core, 3 - 2 * core]
+    line = [y, x]
+    up = (c, lax.rem(z + 1, 4))
+    down = (c, lax.rem(z + 3, 4))
+    sends = []
+
+    def rows_at(k, d, half=None):
+        row = lax.rem(line[k] + d + 4, 4) * 192
+        if half is None:
+            return pl.ds(pl.multiple_of(row, 16), 192)
+        return pl.ds(pl.multiple_of(row + half * 96, 16), 96)
+
+    def start(cp):
+        cp.start()
+        sends.append(cp)
+
+    def scatter(half):
+        for k in range(2):
+            src = w_out.at[rows_at(k, 0, half), pl.ds(pl.multiple_of(quarter[k] * QC, QC), QC)]
+            for slot, dev in ((0, down), (1, up)):
+                i = 4 * half + 2 * k + slot
+                dst = wbuf.at[slot, quarter[k], rows_at(k, 0, half), :]
+                start(remote(src, dst, zs_s.at[i], zs_r.at[i], dev))
+
+    def scattered(half):
+        for k in range(2):
+            for slot in range(2):
+                i = 4 * half + 2 * k + slot
+                dst = wbuf.at[slot, quarter[k], rows_at(k, 0, half), :]
+                remote(dst, dst, zs_s.at[i], zs_r.at[i], sibling).wait_recv()
+
+    def along(k, d):
+        return in_plane(0, d) if k == 0 else in_plane(d, 0)
+
+    def pair(k, d, half, q=None):
+        return wbuf.at[pl.ds(0, 2), quarter[k] if q is None else q, rows_at(k, d, half), :]
+
+    def third(k, d, half=None, q=None):
+        return wbuf.at[2, quarter[k] if q is None else q, rows_at(k, d, half), :]
+
+    def ring_pair(half):
+        for k in range(2):
+            for n, d in enumerate((1, -1)):
+                i = 4 * half + 2 * k + n
+                ref = pair(k, 0, half)
+                start(remote(ref, ref, ra_s.at[i], ra_r.at[i], along(k, d)))
+
+    def ring_third():
+        for k in range(2):
+            for n, d in enumerate((1, -1)):
+                i = 2 * k + n
+                ref = third(k, 0)
+                start(remote(ref, ref, rb_s.at[i], rb_r.at[i], along(k, d)))
+
+    def seq_forward(half):
+        for k in range(2):
+            i = 2 * k + half
+            src = wbuf.at[1 - half, quarter[k], rows_at(k, 0, half), :]
+            dst = third(k, 0, half)
+            start(remote(src, dst, zf_s.at[i], zf_r.at[i], up if half == 0 else down))
+
+    def seq_forwarded():
+        for k in range(2):
+            for half in range(2):
+                i = 2 * k + half
+                ref = third(k, 0, half)
+                remote(ref, ref, zf_s.at[i], zf_r.at[i], sibling).wait_recv()
+
+    def forward_pair(half):
+        for k in range(2):
+            for n, d in enumerate((1, -1)):
+                i = 4 * half + 2 * k + n
+                ref = pair(k, -d, half)
+                remote(ref, ref, ra_s.at[i], ra_r.at[i], sibling).wait_recv()
+                ref = wbuf.at[n, quarter[k], rows_at(k, -d, half), :]
+                start(remote(ref, ref, fa_s.at[i], fa_r.at[i], along(k, d)))
+        for k in range(2):
+            for n, d in enumerate((1, -1)):
+                share(k, pair(k, -d, half), 2 + 3 * n + half)
+
+    def forward_third():
+        for k in range(2):
+            for n, d in enumerate((1, -1)):
+                i = 2 * k + n
+                ref = third(k, -d)
+                remote(ref, ref, rb_s.at[i], rb_r.at[i], sibling).wait_recv()
+                ref = third(k, -d, n)
+                start(remote(ref, ref, fb_s.at[i], fb_r.at[i], along(k, d)))
+        for k in range(2):
+            for n, d in enumerate((1, -1)):
+                share(k, third(k, -d), 4 + 3 * n)
+
+    def opposite_pair(half):
+        for k in range(2):
+            for n, d in enumerate((1, -1)):
+                i = 4 * half + 2 * k + n
+                ref = wbuf.at[n, quarter[k], rows_at(k, 2, half), :]
+                remote(ref, ref, fa_s.at[i], fa_r.at[i], sibling).wait_recv()
+            share(k, pair(k, 2, half), 9 + half)
+
+    def opposite_third():
+        for k in range(2):
+            for n in range(2):
+                i = 2 * k + n
+                ref = third(k, 2, n)
+                remote(ref, ref, fb_s.at[i], fb_r.at[i], sibling).wait_recv()
+            share(k, third(k, 2), 11)
+
+    def share(k, ref, i):
+        start(remote(ref, ref, sib_s.at[12 * k + i], sib_r.at[12 * k + i], sibling))
+
+    def shared(k, d):
+        first = {0: (0, 1, 8), 1: (5, 6, 7), -1: (2, 3, 4), 2: (9, 10, 11)}[d]
+        for n, i in enumerate(first):
+            if n < 2:
+                ref = pair(k, d, n, other[k])
+            else:
+                ref = third(k, d, None, other[k])
+            remote(ref, ref, sib_s.at[12 * k + i], sib_r.at[12 * k + i], sibling).wait_recv()
+
+    scatter(0)
 
     lane = iota((8, 128), 1)
     fzero = jnp.zeros((8, 128), jnp.int32)
@@ -199,30 +308,7 @@
 
     lax.fori_loop(0, 8, act_step, 0)
 
-    for cp in scatter:
-        cp.wait_recv()
-    phase1 = []
-    for k in range(2):
-        for n, d in enumerate((1, -1, 2)):
-            i = k * 3 + n
-            region = wbuf.at[pl.ds(1, 3), quarter[k], pl.ds(piece[k], 48), :]
-            dev = in_plane(d, 0) if k == 0 else in_plane(0, d)
-            cp = remote(region, region, p1_s.at[i], p1_r.at[i], dev)
-            cp.start()
-            phase1.append(cp)
-
-    def wait_phase1():
-        for k in range(2):
-            for n, d in enumerate((1, -1, 2)):
-                i = k * 3 + n
-                if k == 0:
-                    row = y * 192 + lax.rem(x - d + 4, 4) * 48
-                else:
-                    row = x * 192 + lax.rem(y - d + 4, 4) * 48
-                region = wbuf.at[
-                    pl.ds(1, 3), quarter[k], pl.ds(pl.multiple_of(row, 16), 48), :
-                ]
-                remote(region, region, p1_s.at[i], p1_r.at[i], sibling).wait_recv()
+    scatter(1)
 
     for cp in halo:
         cp.wait_recv()
@@ -306,6 +392,12 @@
     lax.fori_loop(0, 32, send_rows, 0)
     precv[c] = pbuf[c]
 
+    scattered(0)
+    ring_pair(0)
+    seq_forward(0)
+    for k in range(2):
+        share(k, pair(k, 0, 0), 0)
+
     loads["wemb"].wait()
     loads["mods"].wait()
     we = wemb[...].astype(F32)
@@ -318,10 +410,11 @@
     shift_b = modv[0, pl.ds(p_own + 32, 1), :]
     lhs[0:64] = (we * scale_a).astype(BF16)
     lhs[64:128] = (we * scale_b).astype(BF16)
+    pad = jnp.zeros((14, D), F32)
     extra = jnp.concatenate(
-        [be * scale_a, shift_a, be * scale_b, shift_b, jnp.zeros((12, D), F32)], axis=0
+        [be * scale_a, shift_a, pad, be * scale_b, shift_b, pad], axis=0
     )
-    lhs[128:144] = extra.astype(BF16)
+    lhs[128:160] = extra.astype(BF16)
     full = jnp.concatenate([we, be, jnp.zeros((63, D), F32)], axis=0)
     hi = full.astype(BF16)
     lo = (full - hi.astype(F32)).astype(BF16)
@@ -335,13 +428,15 @@
         loads[("wq", j)].wait()
         prod = mm(lhs[...], wq[j]).astype(BF16)
         for k in range(2):
-            part = jnp.concatenate([prod[64 * k : 64 * k + 64], prod[128:144]], axis=0)
+            part = jnp.concatenate(
+                [prod[64 * k : 64 * k + 64], prod[128 + 16 * k : 144 + 16 * k]], axis=0
+            )
             if j < 2:
                 mqk[j, k] = part
             else:
                 mb[0, k, 1, 0:80, :] = part
-    for k in range(2):
-        one = jnp.where((bias_row == 65 + 2 * k) & (bias_col == 68), 1.0, 0.0)
+    one = jnp.where((bias_row == 65) & (bias_col == 66), 1.0, 0.0)
+    for k in range(2):
         for h in range(6):
             mq = mqk[0, k, :, 128 * h : 128 * h + 128]
             mk = jnp.concatenate(
@@ -366,35 +461,11 @@
         cp.start()
         mb_send.append(cp)
 
-    wait_phase1()
-    line = [y, x]
-
-    def block(k, d, half=None):
-        row = lax.rem(line[k] + d + 4, 4) * 192
-        size = 192
-        if half is not None:
-            row = row + half * 96
-            size = 96
-        return (pl.ds(1, 3), quarter[k], pl.ds(pl.multiple_of(row, 16), size), slice(None))
-
-    def along(k, d):
-        return in_plane(0, d) if k == 0 else in_plane(d, 0)
-
-    sends = []
-
-    def push(region, ss, rs, dev):
-        cp = remote(wbuf.at[region], wbuf.at[region], ss, rs, dev)
-        cp.start()
-        sends.append(cp)
-
-    def arrived(region, ss, rs):
-        remote(wbuf.at[region], wbuf.at[region], ss, rs, sibling).wait_recv()
-
-    for k in range(2):
-        for n, d in enumerate((1, -1)):
-            push(block(k, 0), p2_s.at[2 * k + n], p2_r.at[2 * k + n], along(k, d))
-    for k in range(2):
-        push(block(k, 0), sib_s.at[4 * k], sib_r.at[4 * k], sibling)
+    scattered(1)
+    ring_pair(1)
+    seq_forward(1)
+    for k in range(2):
+        share(k, pair(k, 0, 1), 1)
 
     def get_rows(s, carry):
         @pl.when(s != c)
@@ -423,6 +494,10 @@
         )
         cp.start()
         pk_send.append(cp)
+    seq_forwarded()
+    ring_third()
+    for k in range(2):
+        share(k, third(k, 0), 8)
     for cp in pk_send:
         cp.wait_recv()
 
@@ -448,10 +523,11 @@
         length = l_a if k == 0 else l_b
         bias = jnp.where(kpos < length, 0.0, -1e30)
         full_row = pt * rstd
-        full_row = jnp.where(klane == 64 + 2 * k, rstd, full_row)
-        full_row = jnp.where(klane == 65 + 2 * k, 1.0, full_row)
-        full_row = jnp.where(klane == 68, bias, full_row)
+        full_row = jnp.where(klane == 64, rstd, full_row)
+        full_row = jnp.where(klane == 65, 1.0, full_row)
+        full_row = jnp.where(klane == 66, bias, full_row)
         keysp[k] = full_row.astype(BF16)
+        keyst[k] = full_row.T.astype(BF16)
 
     trow = iota((256, 256), 0)
     tcol = iota((256, 256), 1)
@@ -468,19 +544,19 @@
         def one_clip(k, carry):
             keys = keysp[k]
             queries = mm(keys[0:128], mb[r, k, 0]).astype(BF16)
-            den_lane = 65 + 2 * k
-            sel = iota((128, 128), 1) == den_lane
-            for h in range(6):
-                s = mm_t(queries[:, 128 * h : 128 * h + 128], keys)
+            for g in range(3):
+                lanes = [256 * g, 256 * g + 128]
+                q2 = jnp.concatenate([queries[:, a : a + 128] for a in lanes], axis=0)
+                s = mm(q2, keyst[k])
                 top = jnp.max(s, axis=1, keepdims=True)
                 w = jnp.exp2(s - top).astype(BF16)
                 rr = mm(w, keys)
-                den = jnp.sum(jnp.where(sel, rr, 0.0), axis=1, keepdims=True)
-                rn = (rr / den).astype(BF16)
-                o = mm(rn, mb[r, k, 1, :, 128 * h : 128 * h + 128])
-                attn_int[pl.ds(pl.multiple_of(128 * k, 128), 128), 128 * h : 128 * h + 128] = (
-                    o.astype(BF16)
-                )
+                rn = (rr * (1.0 / rr[:, 65:66])).astype(BF16)
+                for n, a in enumerate(lanes):
+                    o = mm(rn[128 * n : 128 * n + 128], mb[r, k, 1, :, a : a + 128])
+                    attn_int[pl.ds(pl.multiple_of(128 * k, 128), 128), a : a + 128] = o.astype(
+                        BF16
+                    )
             return carry
 
         lax.fori_loop(0, 2, one_clip, 0)
@@ -488,19 +564,14 @@
 
     attn_own[...] = attend(0)
 
-    for k in range(2):
-        for n, d in enumerate((1, -1)):
-            arrived(block(k, -d), p2_s.at[2 * k + n], p2_r.at[2 * k + n])
-            push(block(k, -d, n), fw_s.at[2 * k + n], fw_r.at[2 * k + n], along(k, d))
-    for k in range(2):
-        for n, d in enumerate((1, -1)):
-            push(block(k, -d), sib_s.at[4 * k + 1 + n], sib_r.at[4 * k + 1 + n], sibling)
-
+    forward_pair(0)
     for q in range(4):
         loads[("wo", q)].wait()
         acc[q] = mm(attn_own[...], wown[q])
-
-    def foreign(r, carry):
+    forward_pair(1)
+
+    def foreign(slot, carry):
+        r = lax.rem(2 * slot, 3) + 1
         remote(
             mb.at[0, :, :, pl.ds(0, 80), :],
             mb.at[r, :, :, pl.ds(0, 80), :],
@@ -510,42 +581,37 @@
         ).wait_recv()
         at_r = attend(r)
         for b in range(4):
-            attn_blk[r - 1, b] = at_r[:, 192 * b : 192 * b + 192]
+            attn_blk[slot, b] = at_r[:, 192 * b : 192 * b + 192]
         return carry
 
-    lax.fori_loop(1, 4, foreign, 0)
+    lax.fori_loop(0, 2, foreign, 0)
+    forward_third()
+    lax.fori_loop(2, 3, foreign, 0)
 
     def project(q, blk):
         rows = pl.ds(pl.multiple_of(blk * 192, 16), 192)
         total = acc[q]
-        for r in range(3):
-            total = total + mm(attn_blk[r, blk], wbuf[r + 1, q, rows, :])
+        for slot in range(3):
+            total = total + mm(attn_blk[slot, blk], wbuf[slot, q, rows, :])
         acc[q] = total
 
-    other = [2 - 2 * core, 3 - 2 * core]
-
-    def from_sibling(k, d, i):
-        row = lax.rem(line[k] + d + 4, 4) * 192
-        region = (pl.ds(1, 3), other[k], pl.ds(pl.multiple_of(row, 16), 192), slice(None))
-        arrived(region, sib_s.at[4 * k + i], sib_r.at[4 * k + i])
-
-    def project_step(k, d, i):
+    def project_step(k, d):
         blk = lax.rem(line[k] + d + 4, 4)
         project(quarter[k], blk)
-        from_sibling(k, d, i)
+        shared(k, d)
         project(other[k], blk)
 
     for k in range(2):
-        project_step(k, 0, 0)
-    for k in range(2):
-        for n, d in enumerate((1, -1)):
-            project_step(k, -d, 1 + n)
-    for k in range(2):
-        for n, d in enumerate((1, -1)):
-            arrived(block(k, 2, n), fw_s.at[2 * k + n], fw_r.at[2 * k + n])
-        push(block(k, 2), sib_s.at[4 * k + 3], sib_r.at[4 * k + 3], sibling)
-    for k in range(2):
-        project_step(k, 2, 3)
+        project_step(k, 0)
+    opposite_pair(0)
+    for k in range(2):
+        project_step(k, -1)
+    opposite_pair(1)
+    for k in range(2):
+        project_step(k, 1)
+    opposite_third()
+    for k in range(2):
+        project_step(k, 2)
 
     orow = iota((256, QC), 0) >> 4
     in_a = orow < l_a
@@ -558,7 +624,7 @@
         )
         out[:, cols] = jnp.where(live, res + gate * acc[q], 0.0).astype(BF16)
 
-    for cp in halo + scatter + phase1 + mb_send + pk_send + sends:
+    for cp in halo + mb_send + pk_send + sends:
         cp.wait_send()
 
     def done_rows(g, carry):
@@ -617,15 +683,16 @@
             pltpu.VMEM((64, D), BF16),
             pltpu.VMEM((3, 64, D), F32),
             pltpu.VMEM((3, D, QC), BF16),
-            pltpu.VMEM((144, D), BF16),
+            pltpu.VMEM((160, D), BF16),
             pltpu.VMEM((2, 2, 80, QC), BF16),
             pltpu.VMEM((4, QC, QC), BF16),
-            pltpu.VMEM((4, 4, QC, QC), BF16),
+            pltpu.VMEM((3, 4, QC, QC), BF16),
             pltpu.VMEM((32, 16, 512), BF16),
             pltpu.VMEM((32, 16, 512), BF16),
             pltpu.VMEM((4, 32, 512), BF16),
             pltpu.VMEM((4, 2, 2, 128, QC), BF16),
             pltpu.VMEM((2, 512, 128), BF16),
+            pltpu.VMEM((2, 128, 512), BF16),
             pltpu.VMEM((256, QC), BF16),
             pltpu.VMEM((256, QC), BF16),
             pltpu.VMEM((3, 4, 256, 192), BF16),
@@ -634,16 +701,20 @@
             dma((11,)),
             dma((2,)),
             dma((2,)),
-            dma((6,)),
-            dma((6,)),
-            dma((6,)),
-            dma((6,)),
-            dma((4,)),
-            dma((4,)),
+            dma((8,)),
+            dma((8,)),
             dma((4,)),
             dma((4,)),
             dma((8,)),
             dma((8,)),
+            dma((4,)),
+            dma((4,)),
+            dma((8,)),
+            dma((8,)),
+            dma((4,)),
+            dma((4,)),
+            dma((24,)),
+            dma((24,)),
             dma((32,)),
             dma((32,)),
             dma((3,)),

time: 96.4 us -> 89.8 us (0.932)
  Pallas kernels: 93.6 us -> 86.9 us
    pallas_call x1, Pallas kernels: 93.6 us -> 86.9 us  [shards(): pl.pallas_call(body, out_shape=jax.ShapeDtypeStruct((256, D), BF16), in_s...]
where the time goes in v2:
time: 89.8 us; the launch traced here: 89.6 us
  Pallas kernels  86.9 us (97%)
  local copies, waits for them, and re-layouts  2.69 us (3%)
    pallas_call x1, Pallas kernels, shards(): pl.pallas_call(body, out_shape=jax.ShapeDtypeStruct((256, D), BF16), in_s...  86.9 us
    unnamed x1, local copies, waits for them, and re-layouts  2.69 us

profile of v2, /device:TPU:1, one launch (start us, length us, event | category | flops | bytes accessed | tf_op | source)
XLA Modules:
  0.0 89.6 jit_solution(13693559548387333412)
XLA Ops:
  0.0 86.9 %shard_map.127 = bf16[256,3072]{1,0:T(8,128)(2,1)} custom-call(bf16[16,64,512]{2,1,0:T(8,128)(2,1)} %bitcast.14, f32[1,512]{1,0:T(1,128)} %bitcast.17, bf16[3,512,512]{2,1,0:T(8,128)(2,1)} %w_conv.1, f32[1,512]{1,0:T(1,128)} %bitcast.18, bf16[16,512]{1,0:T(8,128)(2,1)} %bitcast.15, f32[1,16]{1,0:T(1,128)} %bitcast.19, bf16[64,3072]{1,0:T(8,128)(2,1)} %w_emb.1, ...), custom_call_target="tpu_custom_call" | custom-call | tf_op jit(solution)/shard_map/pallas_call | solution.py:659
  86.9 2.7 %copy.16 = bf16[16,1,16,3072]{3,2,1,0:T(8,128)(2,1)} copy(bf16[16,1,16,3072]{3,2,1,0:T(8,128)(2,1)} %bitcast.12) | data formatting | bytes 3145728

commit v3 on v2

--- a/solution.py
+++ b/solution.py
@@ -410,62 +410,62 @@
     shift_b = modv[0, pl.ds(p_own + 32, 1), :]
     lhs[0:64] = (we * scale_a).astype(BF16)
     lhs[64:128] = (we * scale_b).astype(BF16)
-    pad = jnp.zeros((14, D), F32)
     extra = jnp.concatenate(
-        [be * scale_a, shift_a, pad, be * scale_b, shift_b, pad], axis=0
+        [be * scale_a, shift_a, be * scale_b, shift_b, jnp.zeros((12, D), F32)], axis=0
     )
-    lhs[128:160] = extra.astype(BF16)
-    full = jnp.concatenate([we, be, jnp.zeros((63, D), F32)], axis=0)
-    hi = full.astype(BF16)
-    lo = (full - hi.astype(F32)).astype(BF16)
-    gram = (mm_t(hi, hi) + mm_t(hi, lo) + mm_t(lo, hi)) * (1.0 / D)
-    gram_hi = gram.astype(BF16)
-    gram_lo = (gram - gram_hi.astype(F32)).astype(BF16)
-
-    bias_row = iota((80, 128), 0)
-    bias_col = iota((80, 128), 1)
+    lhs[128:144] = extra.astype(BF16)
+
     for j in range(3):
         loads[("wq", j)].wait()
         prod = mm(lhs[...], wq[j]).astype(BF16)
-        for k in range(2):
-            part = jnp.concatenate(
-                [prod[64 * k : 64 * k + 64], prod[128 + 16 * k : 144 + 16 * k]], axis=0
-            )
-            if j < 2:
-                mqk[j, k] = part
-            else:
-                mb[0, k, 1, 0:80, :] = part
-    one = jnp.where((bias_row == 65) & (bias_col == 66), 1.0, 0.0)
-    for k in range(2):
+        if j < 2:
+            mqk[j] = prod
+        else:
+            mb[0, :, 512:1280] = prod
+    zero64 = jnp.zeros((64, 128), BF16)
+    row128 = iota((128, 128), 0)
+    scale = LOG2E * 128 ** (-0.5)
+    extras = []
+    for k in range(2):
+        def part(j, h):
+            cols = slice(128 * h, 128 * h + 128)
+            return mqk[j, 64 * k : 64 * k + 64, cols]
+
+        def side(h):
+            return jnp.concatenate([part(0, h), mqk[0, 128:144, 128 * h : 128 * h + 128]], axis=0)
+
+        pieces = []
+        column_part = None
+        for p in range(3):
+            even = jnp.concatenate([part(1, 2 * p), zero64], axis=0)
+            odd = jnp.concatenate([zero64, part(1, 2 * p + 1)], axis=0)
+            pieces.append(mm_t(side(2 * p), even) + mm_t(side(2 * p + 1), odd))
         for h in range(6):
-            mq = mqk[0, k, :, 128 * h : 128 * h + 128]
-            mk = jnp.concatenate(
-                [mqk[1, k, :, 128 * h : 128 * h + 128], jnp.zeros((48, 128), BF16)], axis=0
-            )
-            bil = mm_t(mq, mk) * (LOG2E * 128 ** (-0.5)) + one
-            mb[0, k, 0, 0:80, 128 * h : 128 * h + 128] = bil.astype(BF16)
-    zero_rows = jnp.zeros((48, QC), BF16)
-    for r in range(4):
-        for k in range(2):
-            for j in range(2):
-                mb[r, k, j, 80:128, :] = zero_rows
-    mb_send = []
-    for r in range(1, 4):
-        cp = remote(
-            mb.at[0, :, :, pl.ds(0, 80), :],
-            mb.at[r, :, :, pl.ds(0, 80), :],
-            mb_s.at[r - 1],
-            mb_r.at[r - 1],
-            (c, lax.rem(z - r + 4, 4)),
-        )
-        cp.start()
-        mb_send.append(cp)
+            key_bias = mqk[1, 128 + 2 * k : 129 + 2 * k, 128 * h : 128 * h + 128].astype(F32)
+            spread = jnp.where(row128 == h, jnp.broadcast_to(key_bias, (128, 128)), 0.0)
+            term = mm_t(side(h), spread.astype(BF16))
+            column_part = term if column_part is None else column_part + term
+        maps = jnp.concatenate(pieces + [column_part], axis=1) * scale
+        mb[0, 64 * k : 64 * k + 64, 0:512] = maps[0:64].astype(BF16)
+        extras.append(maps[64:80])
+    mb[0, 128:144, 0:512] = jnp.where(iota((16, 512), 0) < 2, extras[0], extras[1]).astype(BF16)
 
     scattered(1)
     ring_pair(1)
     seq_forward(1)
     for k in range(2):
         share(k, pair(k, 0, 1), 1)
+
+    def maps_copy(slot, dev):
+        return remote(mb.at[0], mb.at[slot], mb_s.at[slot - 1], mb_r.at[slot - 1], dev)
+
+    def maps_forward(slot, n, dev):
+        rows = pl.ds(0, 80) if n == 0 else pl.ds(80, 64)
+        src, dst = mb.at[slot, rows, :], mb.at[2, rows, :]
+        return remote(src, dst, mb_s.at[3 + n], mb_r.at[3 + n], dev)
+
+    start(maps_copy(1, down))
+    start(maps_copy(3, up))
 
     def get_rows(s, carry):
         @pl.when(s != c)
@@ -494,10 +494,12 @@
         )
         cp.start()
         pk_send.append(cp)
-    seq_forwarded()
-    ring_third()
-    for k in range(2):
-        share(k, third(k, 0), 8)
+    full = jnp.concatenate([we, be, jnp.zeros((63, D), F32)], axis=0)
+    hi = full.astype(BF16)
+    lo = (full - hi.astype(F32)).astype(BF16)
+    gram = (mm_t(hi, hi) + mm_t(hi, lo) + mm_t(lo, hi)) * (1.0 / D)
+    gram_hi = gram.astype(BF16)
+    gram_lo = (gram - gram_hi.astype(F32)).astype(BF16)
     for cp in pk_send:
         cp.wait_recv()
 
@@ -523,11 +525,13 @@
         length = l_a if k == 0 else l_b
         bias = jnp.where(kpos < length, 0.0, -1e30)
         full_row = pt * rstd
-        full_row = jnp.where(klane == 64, rstd, full_row)
-        full_row = jnp.where(klane == 65, 1.0, full_row)
-        full_row = jnp.where(klane == 66, bias, full_row)
+        full_row = jnp.where(klane == 64 + 2 * k, rstd, full_row)
+        full_row = jnp.where(klane == 65 + 2 * k, 1.0, full_row)
+        full_row = jnp.where(klane == 68, bias, full_row)
         keysp[k] = full_row.astype(BF16)
-        keyst[k] = full_row.T.astype(BF16)
+        keyst[k, 0] = full_row.T.astype(BF16)
+        turned = jnp.concatenate([full_row[:, 64:128], full_row[:, 0:64]], axis=1)
+        keyst[k, 1] = turned.T.astype(BF16)
 
     trow = iota((256, 256), 0)
     tcol = iota((256, 256), 1)
@@ -540,26 +544,32 @@
     perm = perm.astype(F32).astype(BF16)
     ptf[...] = mm(perm, jnp.concatenate(tokens, axis=0)).astype(BF16)
 
+    qlane = iota((128, 128), 1)
+    tail = jnp.zeros((48, 1280), BF16)
+
     def attend(r):
-        def one_clip(k, carry):
+        for k in range(2):
             keys = keysp[k]
-            queries = mm(keys[0:128], mb[r, k, 0]).astype(BF16)
-            for g in range(3):
-                lanes = [256 * g, 256 * g + 128]
-                q2 = jnp.concatenate([queries[:, a : a + 128] for a in lanes], axis=0)
-                s = mm(q2, keyst[k])
+            maps = jnp.concatenate([mb[r, 64 * k : 64 * k + 64], mb[r, 128:144], tail], axis=0)
+            queries = mm(keys[0:128], maps[:, 0:512])
+            for odd in range(2):
+                main = (qlane < 64) if odd == 0 else (qlane >= 64)
+                base = 64 - 64 * odd
+                stack = []
+                for p in range(3):
+                    bias = queries[:, 384 + 2 * p + odd : 385 + 2 * p + odd]
+                    rest = jnp.where(qlane == base + 2 * k, bias, 0.0)
+                    rest = jnp.where(qlane == base + 4, 1.0, rest)
+                    stack.append(jnp.where(main, queries[:, 128 * p : 128 * p + 128], rest))
+                s = mm(jnp.concatenate(stack, axis=0).astype(BF16), keyst[k, odd])
                 top = jnp.max(s, axis=1, keepdims=True)
                 w = jnp.exp2(s - top).astype(BF16)
                 rr = mm(w, keys)
-                rn = (rr * (1.0 / rr[:, 65:66])).astype(BF16)
-                for n, a in enumerate(lanes):
-                    o = mm(rn[128 * n : 128 * n + 128], mb[r, k, 1, :, a : a + 128])
-                    attn_int[pl.ds(pl.multiple_of(128 * k, 128), 128), a : a + 128] = o.astype(
-                        BF16
-                    )
-            return carry
-
-        lax.fori_loop(0, 2, one_clip, 0)
+                rn = (rr * (1.0 / rr[:, 65 + 2 * k : 66 + 2 * k])).astype(BF16)
+                for p in range(3):
+                    a = 128 * (2 * p + odd)
+                    o = mm(rn[128 * p : 128 * p + 128], maps[:, 512 + a : 640 + a])
+                    attn_int[128 * k : 128 * k + 128, a : a + 128] = o.astype(BF16)
         return mm(perm, attn_int[...]).astype(BF16)
 
     attn_own[...] = attend(0)
@@ -568,24 +578,27 @@
     for q in range(4):
         loads[("wo", q)].wait()
         acc[q] = mm(attn_own[...], wown[q])
+    seq_forwarded()
+    ring_third()
+    for k in range(2):
+        share(k, third(k, 0), 8)
     forward_pair(1)
 
+    maps_copy(1, sibling).wait_recv()
+    start(maps_forward(1, 1, down))
+    maps_copy(3, sibling).wait_recv()
+    start(maps_forward(3, 0, up))
+
     def foreign(slot, carry):
-        r = lax.rem(2 * slot, 3) + 1
-        remote(
-            mb.at[0, :, :, pl.ds(0, 80), :],
-            mb.at[r, :, :, pl.ds(0, 80), :],
-            mb_s.at[r - 1],
-            mb_r.at[r - 1],
-            sibling,
-        ).wait_recv()
-        at_r = attend(r)
+        at_r = attend(lax.rem(2 * slot, 3) + 1)
         for b in range(4):
             attn_blk[slot, b] = at_r[:, 192 * b : 192 * b + 192]
         return carry
 
     lax.fori_loop(0, 2, foreign, 0)
     forward_third()
+    for n in range(2):
+        maps_forward(1, n, sibling).wait_recv()
     lax.fori_loop(2, 3, foreign, 0)
 
     def project(q, blk):
@@ -624,7 +637,7 @@
         )
         out[:, cols] = jnp.where(live, res + gate * acc[q], 0.0).astype(BF16)
 
-    for cp in halo + mb_send + pk_send + sends:
+    for cp in halo + pk_send + sends:
         cp.wait_send()
 
     def done_rows(g, carry):
@@ -683,16 +696,16 @@
             pltpu.VMEM((64, D), BF16),
             pltpu.VMEM((3, 64, D), F32),
             pltpu.VMEM((3, D, QC), BF16),
-            pltpu.VMEM((160, D), BF16),
-            pltpu.VMEM((2, 2, 80, QC), BF16),
+            pltpu.VMEM((144, D), BF16),
+            pltpu.VMEM((2, 144, QC), BF16),
             pltpu.VMEM((4, QC, QC), BF16),
             pltpu.VMEM((3, 4, QC, QC), BF16),
             pltpu.VMEM((32, 16, 512), BF16),
             pltpu.VMEM((32, 16, 512), BF16),
             pltpu.VMEM((4, 32, 512), BF16),
-            pltpu.VMEM((4, 2, 2, 128, QC), BF16),
+            pltpu.VMEM((4, 144, 1280), BF16),
             pltpu.VMEM((2, 512, 128), BF16),
-            pltpu.VMEM((2, 128, 512), BF16),
+            pltpu.VMEM((2, 2, 128, 512), BF16),
             pltpu.VMEM((256, QC), BF16),
             pltpu.VMEM((256, QC), BF16),
             pltpu.VMEM((3, 4, 256, 192), BF16),
@@ -717,8 +730,8 @@
             dma((24,)),
             dma((32,)),
             dma((32,)),
-            dma((3,)),
-            dma((3,)),
+            dma((5,)),
+            dma((5,)),
             dma((3,)),
             dma((3,)),
         ],

time: 89.8 us -> 77.8 us (0.87)
  Pallas kernels: 86.9 us -> 74.9 us
    pallas_call x1, Pallas kernels: 86.9 us -> 74.9 us  [shards(): pl.pallas_call(body, out_shape=jax.ShapeDtypeStruct((256, D), BF16), in_s...]
where the time goes in v3:
time: 77.8 us; the launch traced here: 77.6 us
  Pallas kernels  74.9 us (96%)
  local copies, waits for them, and re-layouts  2.69 us (3%)
    pallas_call x1, Pallas kernels, shards(): pl.pallas_call(body, out_shape=jax.ShapeDtypeStruct((256, D), BF16), in_s...  74.9 us
    unnamed x1, local copies, waits for them, and re-layouts  2.69 us

profile of v3, /device:TPU:1, one launch (start us, length us, event | category | flops | bytes accessed | tf_op | source)
XLA Modules:
  0.0 77.6 jit_solution(5239566753189916770)
XLA Ops:
  0.0 74.9 %shard_map.127 = bf16[256,3072]{1,0:T(8,128)(2,1)} custom-call(bf16[16,64,512]{2,1,0:T(8,128)(2,1)} %bitcast.14, f32[1,512]{1,0:T(1,128)} %bitcast.17, bf16[3,512,512]{2,1,0:T(8,128)(2,1)} %w_conv.1, f32[1,512]{1,0:T(1,128)} %bitcast.18, bf16[16,512]{1,0:T(8,128)(2,1)} %bitcast.15, f32[1,16]{1,0:T(1,128)} %bitcast.19, bf16[64,3072]{1,0:T(8,128)(2,1)} %w_emb.1, ...), custom_call_target="tpu_custom_call" | custom-call | tf_op jit(solution)/shard_map/pallas_call | solution.py:672
  74.9 2.7 %copy.16 = bf16[16,1,16,3072]{3,2,1,0:T(8,128)(2,1)} copy(bf16[16,1,16,3072]{3,2,1,0:T(8,128)(2,1)} %bitcast.12) | data formatting | bytes 3145728

commit v4 on v3

--- a/solution.py
+++ b/solution.py
@@ -116,8 +116,6 @@
     load("mods", mods, modv, 3)
     for j in range(3):
         load(("wq", j), w_qkv.at[j], wq.at[j], 4 + j)
-    for q in range(4):
-        load(("wo", q), w_out.at[:, pl.ds(q * QC, QC)], wown.at[q], 7 + q)
 
     barrier = pltpu.get_barrier_semaphore()
 
@@ -133,16 +131,6 @@
         pl.semaphore_signal(
             barrier, inc=1, device_id=(c, lax.rem(z + r, 4)), device_id_type=MESH
         )
-    pl.semaphore_wait(barrier, 34)
-
-    nxt = (lax.rem(c + 1, 32), z)
-    prv = (lax.rem(c + 31, 32), z)
-    halo = [
-        remote(vae.at[pl.ds(15, 1)], xin.at[pl.ds(0, 1)], halo_s.at[0], halo_r.at[0], nxt),
-        remote(vae.at[pl.ds(0, 1)], xin.at[pl.ds(17, 1)], halo_s.at[1], halo_r.at[1], prv),
-    ]
-    for cp in halo:
-        cp.start()
 
     quarter = [2 * core, 2 * core + 1]
     other = [2 - 2 * core, 3 - 2 * core]
@@ -256,16 +244,16 @@
     def share(k, ref, i):
         start(remote(ref, ref, sib_s.at[12 * k + i], sib_r.at[12 * k + i], sibling))
 
-    def shared(k, d):
+    def shared(k, d, slots):
         first = {0: (0, 1, 8), 1: (5, 6, 7), -1: (2, 3, 4), 2: (9, 10, 11)}[d]
         for n, i in enumerate(first):
+            if (n == 2 and 2 not in slots) or (n < 2 and 0 not in slots):
+                continue
             if n < 2:
                 ref = pair(k, d, n, other[k])
             else:
                 ref = third(k, d, None, other[k])
             remote(ref, ref, sib_s.at[12 * k + i], sib_r.at[12 * k + i], sibling).wait_recv()
-
-    scatter(0)
 
     lane = iota((8, 128), 1)
     fzero = jnp.zeros((8, 128), jnp.int32)
@@ -308,12 +296,44 @@
 
     lax.fori_loop(0, 8, act_step, 0)
 
-    scatter(1)
+    loads["wemb"].wait()
+    loads["mods"].wait()
+    we = wemb[...].astype(F32)
+    we = we - jnp.mean(we, axis=1, keepdims=True)
+    be = b_emb[...]
+    be = be - jnp.mean(be, axis=1, keepdims=True)
+    scale_a = 1.0 + modv[1, pl.ds(p_own, 1), :]
+    scale_b = 1.0 + modv[1, pl.ds(p_own + 32, 1), :]
+    shift_a = modv[0, pl.ds(p_own, 1), :]
+    shift_b = modv[0, pl.ds(p_own + 32, 1), :]
+    lhs[0:64] = (we * scale_a).astype(BF16)
+    lhs[64:128] = (we * scale_b).astype(BF16)
+    extra = jnp.concatenate(
+        [be * scale_a, shift_a, be * scale_b, shift_b, jnp.zeros((12, D), F32)], axis=0
+    )
+    lhs[128:144] = extra.astype(BF16)
+
+    pl.semaphore_wait(barrier, 34)
+
+    nxt = (lax.rem(c + 1, 32), z)
+    prv = (lax.rem(c + 31, 32), z)
+    halo = [
+        remote(vae.at[pl.ds(15, 1)], xin.at[pl.ds(0, 1)], halo_s.at[0], halo_r.at[0], nxt),
+        remote(vae.at[pl.ds(0, 1)], xin.at[pl.ds(17, 1)], halo_s.at[1], halo_r.at[1], prv),
+    ]
+    for cp in halo:
+        cp.start()
+
+    scatter(0)
 
     for cp in halo:
         cp.wait_recv()
     act[pl.ds(0, 1)] = activate(xin[pl.ds(0, 1)])
     act[pl.ds(17, 1)] = activate(xin[pl.ds(17, 1)])
+
+    scatter(1)
+    for q in range(4):
+        load(("wo", q), w_out.at[:, pl.ds(q * QC, QC)], wown.at[q], 7 + q)
 
     loads["wconv"].wait()
     fid = c * 16 + iota((16, 128), 0)
@@ -392,29 +412,6 @@
     lax.fori_loop(0, 32, send_rows, 0)
     precv[c] = pbuf[c]
 
-    scattered(0)
-    ring_pair(0)
-    seq_forward(0)
-    for k in range(2):
-        share(k, pair(k, 0, 0), 0)
-
-    loads["wemb"].wait()
-    loads["mods"].wait()
-    we = wemb[...].astype(F32)
-    we = we - jnp.mean(we, axis=1, keepdims=True)
-    be = b_emb[...]
-    be = be - jnp.mean(be, axis=1, keepdims=True)
-    scale_a = 1.0 + modv[1, pl.ds(p_own, 1), :]
-    scale_b = 1.0 + modv[1, pl.ds(p_own + 32, 1), :]
-    shift_a = modv[0, pl.ds(p_own, 1), :]
-    shift_b = modv[0, pl.ds(p_own + 32, 1), :]
-    lhs[0:64] = (we * scale_a).astype(BF16)
-    lhs[64:128] = (we * scale_b).astype(BF16)
-    extra = jnp.concatenate(
-        [be * scale_a, shift_a, be * scale_b, shift_b, jnp.zeros((12, D), F32)], axis=0
-    )
-    lhs[128:144] = extra.astype(BF16)
-
     for j in range(3):
         loads[("wq", j)].wait()
         prod = mm(lhs[...], wq[j]).astype(BF16)
@@ -450,11 +447,11 @@
         extras.append(maps[64:80])
     mb[0, 128:144, 0:512] = jnp.where(iota((16, 512), 0) < 2, extras[0], extras[1]).astype(BF16)
 
-    scattered(1)
-    ring_pair(1)
-    seq_forward(1)
+    scattered(0)
+    ring_pair(0)
+    seq_forward(0)
     for k in range(2):
-        share(k, pair(k, 0, 1), 1)
+        share(k, pair(k, 0, 0), 0)
 
     def maps_copy(slot, dev):
         return remote(mb.at[0], mb.at[slot], mb_s.at[slot - 1], mb_r.at[slot - 1], dev)
@@ -494,6 +491,12 @@
         )
         cp.start()
         pk_send.append(cp)
+    scattered(1)
+    ring_pair(1)
+    seq_forward(1)
+    for k in range(2):
+        share(k, pair(k, 0, 1), 1)
+
     full = jnp.concatenate([we, be, jnp.zeros((63, D), F32)], axis=0)
     hi = full.astype(BF16)
     lo = (full - hi.astype(F32)).astype(BF16)
@@ -502,6 +505,11 @@
     gram_lo = (gram - gram_hi.astype(F32)).astype(BF16)
     for cp in pk_send:
         cp.wait_recv()
+
+    seq_forwarded()
+    ring_third()
+    for k in range(2):
+        share(k, third(k, 0), 8)
 
     klane = iota((512, 128), 1)
     kpos = iota((512, 128), 0) & 7
@@ -578,10 +586,6 @@
     for q in range(4):
         loads[("wo", q)].wait()
         acc[q] = mm(attn_own[...], wown[q])
-    seq_forwarded()
-    ring_third()
-    for k in range(2):
-        share(k, third(k, 0), 8)
     forward_pair(1)
 
     maps_copy(1, sibling).wait_recv()
@@ -596,35 +600,36 @@
         return carry
 
     lax.fori_loop(0, 2, foreign, 0)
+
+    def project(q, blk, slots):
+        rows = pl.ds(pl.multiple_of(blk * 192, 16), 192)
+        total = acc[q]
+        for slot in slots:
+            total = total + mm(attn_blk[slot, blk], wbuf[slot, q, rows, :])
+        acc[q] = total
+
+    def project_step(k, d, slots):
+        blk = lax.rem(line[k] + d + 4, 4)
+        project(quarter[k], blk, slots)
+        shared(k, d, slots)
+        project(other[k], blk, slots)
+
+    for k in range(2):
+        project_step(k, 0, (0, 1))
     forward_third()
     for n in range(2):
         maps_forward(1, n, sibling).wait_recv()
     lax.fori_loop(2, 3, foreign, 0)
-
-    def project(q, blk):
-        rows = pl.ds(pl.multiple_of(blk * 192, 16), 192)
-        total = acc[q]
-        for slot in range(3):
-            total = total + mm(attn_blk[slot, blk], wbuf[slot, q, rows, :])
-        acc[q] = total
-
-    def project_step(k, d):
-        blk = lax.rem(line[k] + d + 4, 4)
-        project(quarter[k], blk)
-        shared(k, d)
-        project(other[k], blk)
-
     for k in range(2):
-        project_step(k, 0)
+        project_step(k, 0, (2,))
     opposite_pair(0)
-    for k in range(2):
-        project_step(k, -1)
     opposite_pair(1)
-    for k in range(2):
-        project_step(k, 1)
+    for d in (1, -1):
+        for k in range(2):
+            project_step(k, d, (0, 1, 2))
     opposite_third()
     for k in range(2):
-        project_step(k, 2)
+        project_step(k, 2, (0, 1, 2))
 
     orow = iota((256, QC), 0) >> 4
     in_a = orow < l_a

time: 77.8 us -> 74.8 us (0.961)
  Pallas kernels: 74.9 us -> 71.9 us
    pallas_call x1, Pallas kernels: 74.9 us -> 71.9 us  [shards(): pl.pallas_call(body, out_shape=jax.ShapeDtypeStruct((256, D), BF16), in_s...]
where the time goes in v4:
time: 74.8 us; the launch traced here: 74.6 us
  Pallas kernels  71.9 us (96%)
  local copies, waits for them, and re-layouts  2.69 us (4%)
    pallas_call x1, Pallas kernels, shards(): pl.pallas_call(body, out_shape=jax.ShapeDtypeStruct((256, D), BF16), in_s...  71.9 us
    unnamed x1, local copies, waits for them, and re-layouts  2.69 us

profile of v4, /device:TPU:1, one launch (start us, length us, event | category | flops | bytes accessed | tf_op | source)
XLA Modules:
  0.0 74.6 jit_solution(18335985375838812439)
XLA Ops:
  0.0 71.9 %shard_map.127 = bf16[256,3072]{1,0:T(8,128)(2,1)} custom-call(bf16[16,64,512]{2,1,0:T(8,128)(2,1)} %bitcast.14, f32[1,512]{1,0:T(1,128)} %bitcast.17, bf16[3,512,512]{2,1,0:T(8,128)(2,1)} %w_conv.1, f32[1,512]{1,0:T(1,128)} %bitcast.18, bf16[16,512]{1,0:T(8,128)(2,1)} %bitcast.15, f32[1,16]{1,0:T(1,128)} %bitcast.19, bf16[64,3072]{1,0:T(8,128)(2,1)} %w_emb.1, ...), custom_call_target="tpu_custom_call" | custom-call | tf_op jit(solution)/shard_map/pallas_call | solution.py:677
  71.9 2.7 %copy.16 = bf16[16,1,16,3072]{3,2,1,0:T(8,128)(2,1)} copy(bf16[16,1,16,3072]{3,2,1,0:T(8,128)(2,1)} %bitcast.12) | data formatting | bytes 3145728
